TPU v7x, 32 devices: a whole 2x2x4 slice. The times are simulated.
32 devices in a mesh: groups: 2 (over y), ctx: 4 (over z), exp: 2 (over x), tp: 2 (over core).
Axes of the slice: x: 2, y: 2, z: 4, core: 2. Of those that a mesh axis runs over, the one named last changes fastest.
Arguments:
- tokens: bfloat16 [1024, 3072], P(('groups', 'ctx')), parts along dimension 0, may hold values from -6 to 6
- out_grad: bfloat16 [1024, 3072], P(('groups', 'ctx')), parts along dimension 0, may hold values from -6 to 6
- expert_ids: int32 [1024, 2], P(('groups', 'ctx')), parts along dimension 0, may hold values from 0 to 3, all different within a row; in each aligned block of 128 rows (0 to 127, 128 to 255, ...) at most 72 rows name the same one
- gate_weights: float32 [1024, 2], P(('groups', 'ctx')), parts along dimension 0, may hold values from 0.1 to 1
- gate_matrix: bfloat16 [4, 3072, 8192], P('exp', None, ('ctx', 'tp')), may hold values from -0.109375 to 0.109375
- up_matrix: bfloat16 [4, 3072, 8192], P('exp', None, ('ctx', 'tp')), may hold values from -0.109375 to 0.109375
- down_matrix: bfloat16 [4, 8192, 3072], P('exp', ('ctx', 'tp')), may hold values from -0.0625 to 0.0625
Outputs:
- grad_gate: bfloat16 [8, 3072, 8192], P(('groups', 'exp'), None, ('ctx', 'tp')), parts along dimension 0
- grad_up: bfloat16 [8, 3072, 8192], P(('groups', 'exp'), None, ('ctx', 'tp')), parts along dimension 0
- grad_down: bfloat16 [8, 8192, 3072], P(('groups', 'exp'), ('ctx', 'tp')), parts along dimension 0
- grad_tokens: bfloat16 [1024, 3072], P(('groups', 'ctx'), ('exp', 'tp')), parts along dimension 0
There are 2 independent parts, one for each index of `groups`. A program takes and returns all parts, laid end to end along the dimension named above; an argument that names none is the same for every part. Nothing has to cross between parts.
Inputs may be any that keep to these rules, and one draw needn't show every extreme that they name: `expert_ids`: the 2 experts of a token differ; among the 128 tokens of one aligned block at most 72 name any one expert.
All inputs are finite; a program needn't handle non-finite values.
Results may differ from a plain program's by a relative error of at most 0.014.
Values may be sent and summed in bfloat16 or wider, within the bound.
No kernel may reach another device: no remote copies, remote signals or barrier semaphores. Data moves between devices by JAX's collectives and lax.ppermute only.
A program may use at most 192 MiB of HBM per device.

v0:
```python
import jax
import jax.numpy as jnp
from jax import lax
from jax.sharding import PartitionSpec as P

CAP = 72


def pack_block(block_ids, block_gates, block_tokens, block_grads, expert):
    rows_here = block_tokens.shape[0]
    chosen = block_ids == expert
    member = jnp.any(chosen, axis=1)
    weight = jnp.sum(jnp.where(chosen, block_gates, jnp.zeros_like(block_gates)), axis=1)
    order_index = jnp.cumsum(member.astype(jnp.int32)) - 1
    slot_ids = jnp.arange(CAP, dtype=jnp.int32)
    positions = jnp.arange(rows_here, dtype=jnp.int32)
    match = jnp.logical_and(member[None, :], order_index[None, :] == slot_ids[:, None])
    filled = jnp.any(match, axis=1)
    source = jnp.sum(jnp.where(match, positions[None, :], 0), axis=1)
    source = source + jnp.where(filled, 0, rows_here).astype(jnp.int32)
    scaled = (weight[:, None] * block_grads.astype(jnp.float32)).astype(jnp.bfloat16)
    zero_row = jnp.zeros((1, block_tokens.shape[1]), jnp.bfloat16)
    packed_tokens = jnp.take(jnp.concatenate([block_tokens, zero_row], axis=0), source, axis=0)
    packed_grads = jnp.take(jnp.concatenate([scaled, zero_row], axis=0), source, axis=0)
    home_slot = jnp.where(member, order_index, CAP)
    return (packed_tokens, packed_grads, home_slot)


def per_device(tokens, out_grad, expert_ids, gate_weights, gate_matrix, up_matrix, down_matrix):
    local_count = gate_matrix.shape[0]
    model_width = tokens.shape[1]
    token_count = tokens.shape[0]
    first_expert = lax.axis_index("exp") * local_count
    packed = [
        pack_block(expert_ids, gate_weights, tokens, out_grad, first_expert + local)
        for local in range(local_count)
    ]
    local_tokens = jnp.stack([item[0] for item in packed], axis=0)
    local_grads = jnp.stack([item[1] for item in packed], axis=0)
    home_slots = [item[2] for item in packed]
    all_tokens, all_grads = (
        lax.all_gather(local_tokens, "ctx", axis=1, tiled=True),
        lax.all_gather(local_grads, "ctx", axis=1, tiled=True),
    )
    slot_total = all_tokens.shape[1]
    gate_grads = []
    up_grads = []
    grad_gate_list = []
    grad_up_list = []
    grad_down_list = []
    for local in range(local_count):
        rows_in = all_tokens[local]
        grads_in = all_grads[local]
        gate_pre = jnp.dot(rows_in, gate_matrix[local], preferred_element_type=jnp.float32)
        up_pre = jnp.dot(rows_in, up_matrix[local], preferred_element_type=jnp.float32)
        sig = jax.nn.sigmoid(gate_pre)
        act = gate_pre * sig
        hidden = (act * up_pre).astype(jnp.bfloat16)
        hidden_grad = jnp.dot(grads_in, down_matrix[local].T, preferred_element_type=jnp.float32)
        up_grad = (hidden_grad * act).astype(jnp.bfloat16)
        gate_grad = (hidden_grad * up_pre * sig * (1.0 + gate_pre * (1.0 - sig))).astype(
            jnp.bfloat16
        )
        gate_grads.append(gate_grad)
        up_grads.append(up_grad)
        grad_down_list.append(
            jnp.dot(hidden.T, grads_in, preferred_element_type=jnp.float32).astype(jnp.bfloat16)
        )
        grad_gate_list.append(
            jnp.dot(rows_in.T, gate_grad, preferred_element_type=jnp.float32).astype(jnp.bfloat16)
        )
        grad_up_list.append(
            jnp.dot(rows_in.T, up_grad, preferred_element_type=jnp.float32).astype(jnp.bfloat16)
        )
    exp_count = lax.axis_size("exp")
    tp_count = lax.axis_size("tp")
    slab_width = model_width // (exp_count * tp_count)
    terms = []
    for partial_local in range(local_count):
        gate_part = gate_grads[partial_local]
        up_part = up_grads[partial_local]
        term = jnp.dot(gate_part, gate_matrix[partial_local].T, preferred_element_type=jnp.float32)
        term = term + jnp.dot(
            up_part, up_matrix[partial_local].T, preferred_element_type=jnp.float32
        )
        terms.append(term)
    complete = jnp.stack(terms, axis=1).reshape(
        slot_total, local_count, exp_count, tp_count, slab_width
    )
    halved = lax.psum_scatter(complete.astype(jnp.bfloat16), "tp", scatter_dimension=3, tiled=True)
    mine_rows = lax.psum_scatter(halved, "ctx", scatter_dimension=0, tiled=True).astype(jnp.float32)
    summed = jnp.zeros((token_count, exp_count, 1, slab_width), jnp.float32)
    for local in range(local_count):
        padded = jnp.concatenate(
            [mine_rows[:, local], jnp.zeros((1, exp_count, 1, slab_width), jnp.float32)], axis=0
        )
        summed = summed + jnp.take(padded, home_slots[local], axis=0)
    reduced = lax.psum_scatter(
        summed.astype(jnp.bfloat16), "exp", scatter_dimension=1, tiled=True
    ).astype(jnp.float32)
    grad_tokens = reduced.reshape(token_count, slab_width).astype(jnp.bfloat16)
    grad_gate = jnp.stack(grad_gate_list, axis=0)
    grad_up = jnp.stack(grad_up_list, axis=0)
    grad_down = jnp.stack(grad_down_list, axis=0)
    return (grad_gate, grad_up, grad_down, grad_tokens)


def solution(mesh):
    in_specs = (
        P(("groups", "ctx"), None),
        P(("groups", "ctx"), None),
        P(("groups", "ctx"), None),
        P(("groups", "ctx"), None),
        P("exp", None, ("ctx", "tp")),
        P("exp", None, ("ctx", "tp")),
        P("exp", ("ctx", "tp"), None),
    )
    out_specs = (
        P(("groups", "exp"), None, ("ctx", "tp")),
        P(("groups", "exp"), None, ("ctx", "tp")),
        P(("groups", "exp"), ("ctx", "tp"), None),
        P(("groups", "ctx"), ("exp", "tp")),
    )
    return jax.shard_map(
        per_device, mesh=mesh, in_specs=in_specs, out_specs=out_specs, check_vma=False
    )
```

profile of v0, /device:TPU:0, one launch (start us, length us, event | category | flops | bytes accessed | tf_op | source)
XLA Modules:
  0.0 299.0 jit_solution(3969634083703119786)
XLA Ops:
  17.3 71.7 %all-gather.3.cloned.1.call-done = bf16[2,288,3072]{2,1,0:T(8,128)(2,1)} async-done(((bf16[2,72,3072]{2,1,0:T(8,128)(2,1)}), bf16[2,288,3072]{2,1,0:T(8,128)(2,1)}) %all-gather.3.cloned.1.call-update) | async-done | bytes 3538960 | tf_op jit(solution)/shard_map/all_gather | solution.py:42
  89.0 5.5 %fusion.2 = f32[288,1024]{1,0:T(8,128)S(1)} fusion(bf16[2,3072,1024]{2,1,0:T(8,128)(2,1)} %param.15, bf16[2,288,3072]{2,1,0:T(8,128)(2,1)} %all-gather.3.cloned.1.call-done), kind=kOutput, calls=%fused_computation.11 | convolution fusion | flops 1811939328 | bytes 9240576 | tf_op jit(solution)/shard_map/dot_general | solution.py:54
  94.5 5.7 %fusion.6 = f32[288,1024]{1,0:T(8,128)S(1)} fusion(bf16[2,3072,1024]{2,1,0:T(8,128)(2,1)} %param.16, bf16[2,288,3072]{2,1,0:T(8,128)(2,1)S(1)} %copy-done.1), kind=kOutput, calls=%fused_computation.15 | convolution fusion | flops 1811939328 | bytes 9240576 | tf_op jit(solution)/shard_map/dot_general | solution.py:55
  100.2 59.5 %all-gather.5.cloned.1.call-done = bf16[2,288,3072]{2,1,0:T(8,128)(2,1)} async-done(((bf16[2,72,3072]{2,1,0:T(8,128)(2,1)}), bf16[2,288,3072]{2,1,0:T(8,128)(2,1)}) %all-gather.5.cloned.1.call-update) | async-done | bytes 3538960 | tf_op jit(solution)/shard_map/all_gather | solution.py:43
  159.7 5.6 %multiply_convert_fusion.2 = (bf16[288,1024]{1,0:T(8,128)(2,1)S(1)}, bf16[288,1024]{1,0:T(8,128)(2,1)S(1)}) fusion(f32[288,1024]{1,0:T(8,128)S(1)} %fusion.2, f32[288,1024]{1,0:T(8,128)S(1)} %fusion.6, bf16[2,1024,3072]{2,1,0:T(8,128)(2,1)} %param.17, bf16[2,288,3072]{2,1,0:T(8,128)(2,1)} %all-gather.5.cloned.1.call-done), kind=kOutput, calls=%fused_computation.61 | convolution fusion | flops 1815773184 | bytes 11599872 | tf_op jit(solution)/shard_map/dot_general | solution.py:59
  165.4 5.3 %fusion = f32[288,3072]{1,0:T(8,128)S(1)} fusion(bf16[288,1024]{1,0:T(8,128)(2,1)S(1)} %get-tuple-element.21, bf16[2,3072,1024]{2,1,0:T(8,128)(2,1)} %param.15), kind=kOutput, calls=%fused_computation.9 | convolution fusion | flops 1811939328 | bytes 10420224 | tf_op jit(solution)/shard_map/dot_general | solution.py:82
  170.7 4.9 %fusion.36 = bf16[288,3072]{1,0:T(8,128)(2,1)S(1)} fusion(f32[288,3072]{1,0:T(8,128)S(1)} %fusion, bf16[288,1024]{1,0:T(8,128)(2,1)S(1)} %get-tuple-element.20, bf16[2,3072,1024]{2,1,0:T(8,128)(2,1)} %param.16), kind=kOutput, calls=%fused_computation.47 | convolution fusion | flops 1813708800 | bytes 12189696 | tf_op jit(solution)/shard_map/dot_general | solution.py:83
  175.6 1.6 stack.70
  177.5 5.5 %fusion.12 = f32[288,1024]{1,0:T(8,128)S(1)} fusion(bf16[2,3072,1024]{2,1,0:T(8,128)(2,1)} %param.15, bf16[2,288,3072]{2,1,0:T(8,128)(2,1)} %all-gather.3.cloned.1.call-done), kind=kOutput, calls=%fused_computation.21 | convolution fusion | flops 1811939328 | bytes 9240576 | tf_op jit(solution)/shard_map/dot_general | solution.py:54
  183.0 6.5 %fusion.16 = f32[288,1024]{1,0:T(8,128)} fusion(bf16[2,3072,1024]{2,1,0:T(8,128)(2,1)} %param.16, bf16[2,288,3072]{2,1,0:T(8,128)(2,1)S(1)} %copy-done.2), kind=kOutput, calls=%fused_computation.25 | convolution fusion | flops 1811939328 | bytes 9240576 | tf_op jit(solution)/shard_map/dot_general | solution.py:55
  189.5 5.0 %multiply_convert_fusion.3 = (bf16[288,1024]{1,0:T(8,128)(2,1)}, bf16[288,1024]{1,0:T(8,128)(2,1)S(1)}) fusion(f32[288,1024]{1,0:T(8,128)S(1)} %fusion.12, f32[288,1024]{1,0:T(8,128)} %fusion.16, bf16[2,1024,3072]{2,1,0:T(8,128)(2,1)S(1)} %bitcast.126, bf16[2,288,3072]{2,1,0:T(8,128)(2,1)} %all-gather.5.cloned.1.call-done), kind=kOutput, calls=%fused_computation.62 | convolution fusion | flops 1815773184 | bytes 11599872 | tf_op jit(solution)/shard_map/dot_general | solution.py:59
  194.6 2.0 fusion.10
  196.7 6.1 %fusion.39 = bf16[288,3072]{1,0:T(8,128)(2,1)} fusion(f32[288,3072]{1,0:T(8,128)S(1)} %fusion.10, bf16[288,1024]{1,0:T(8,128)(2,1)S(1)} %copy-done.16, bf16[2,3072,1024]{2,1,0:T(8,128)(2,1)} %param.16), kind=kOutput, calls=%fused_computation.48 | convolution fusion | flops 1813708800 | bytes 12189696 | tf_op jit(solution)/shard_map/dot_general | solution.py:83
  202.8 4.4 %stack.69 = bf16[288,1,2,2,768]{4,3,2,0,1:T(2,128)(2,1)S(1)} reshape(bf16[288,3072]{1,0:T(8,128)(2,1)} %fusion.39) | data formatting | bytes 3538944 | tf_op jit(solution)/shard_map/stack | solution.py:87
  207.4 2.1 pad_maximum_fusion.3
  209.7 10.1 %reduce-scatter.7.cloned.1.call-done = bf16[288,2,2,1,768]{4,0,2,1,3:T(8,128)(2,1)} async-done(((bf16[288,2,2,2,768]{4,0,2,1,3:T(8,128)(2,1)}), bf16[288,2,2,1,768]{4,0,2,1,3:T(8,128)(2,1)}) %reduce-scatter.7.cloned.1.call-update) | async-done | bytes 1769488 | tf_op jit(solution)/shard_map/reduce_scatter | solution.py:90
  219.8 3.3 %copy.47 = bf16[288,2,2,1,768]{4,2,3,1,0:T(2,128)(2,1)S(1)} copy(bf16[288,2,2,1,768]{4,0,2,1,3:T(8,128)(2,1)} %reduce-scatter.7.cloned.1.call-done) | data formatting | bytes 3538944
  223.1 2.5 reshape.167
  225.6 9.9 %reduce-scatter.9.cloned.1.call-start = ((), (), s32[]{:S(2)}) async-start(), calls=%async_computation.6 | async-start | bytes 589824 | tf_op jit(solution)/shard_map/reduce_scatter | solution.py:98
  235.6 5.4 %convert_bitcast_fusion.3 = bf16[1,3072,1024]{2,1,0:T(8,128)(2,1)S(1)} fusion(bf16[288,1024]{1,0:T(8,128)(2,1)S(1)} %copy-done.17, bf16[2,288,3072]{2,1,0:T(8,128)(2,1)} %all-gather.3.cloned.1.call-done), kind=kOutput, calls=%fused_computation.32 | convolution fusion | flops 1815085056 | bytes 8650752 | tf_op jit(solution)/shard_map/dot_general | solution.py:73
  240.9 5.4 %convert_bitcast_fusion.5 = bf16[1,3072,1024]{2,1,0:T(8,128)(2,1)} fusion(bf16[288,1024]{1,0:T(8,128)(2,1)S(1)} %copy-done.8, bf16[2,288,3072]{2,1,0:T(8,128)(2,1)S(1)} %copy-done.3), kind=kOutput, calls=%fused_computation.35 | convolution fusion | flops 1815085056 | bytes 8650752 | tf_op jit(solution)/shard_map/dot_general | solution.py:70
  246.3 3.7 %convert_bitcast_fusion.2 = bf16[1,3072,1024]{2,1,0:T(8,128)(2,1)S(1)} fusion(bf16[288,1024]{1,0:T(8,128)(2,1)S(1)} %copy-done.15, bf16[2,288,3072]{2,1,0:T(8,128)(2,1)S(1)} %copy-done.3), kind=kOutput, calls=%fused_computation.31 | convolution fusion | flops 1815085056 | bytes 8650752 | tf_op jit(solution)/shard_map/dot_general | solution.py:73
  250.1 3.8 %convert_bitcast_fusion = bf16[1,1024,3072]{2,1,0:T(8,128)(2,1)S(1)} fusion(bf16[2,288,3072]{2,1,0:T(8,128)(2,1)S(1)} %copy-done.4, f32[288,1024]{1,0:T(8,128)S(1)} %copy-done.12, f32[288,1024]{1,0:T(8,128)S(1)} %copy-done.10), kind=kOutput, calls=%fused_computation.29 | convolution fusion | flops 1816854528 | bytes 10420224 | tf_op jit(solution)/shard_map/dot_general | solution.py:67
  253.9 5.4 %convert_bitcast_fusion.1 = bf16[1,1024,3072]{2,1,0:T(8,128)(2,1)S(1)} fusion(bf16[2,288,3072]{2,1,0:T(8,128)(2,1)S(1)} %copy-done.4, f32[288,1024]{1,0:T(8,128)} %fusion.16, f32[288,1024]{1,0:T(8,128)} %copy-done.13), kind=kOutput, calls=%fused_computation.30 | convolution fusion | flops 1816854528 | bytes 10420224 | tf_op jit(solution)/shard_map/dot_general | solution.py:67
  259.4 5.2 %pad_maximum_fusion.2 = bf16[2,1024,3072]{2,1,0:T(8,128)(2,1)} fusion(bf16[1,1024,3072]{2,1,0:T(8,128)(2,1)S(1)} %convert_bitcast_fusion, bf16[1,1024,3072]{2,1,0:T(8,128)(2,1)S(1)} %convert_bitcast_fusion.1), kind=kLoop, calls=%fused_computation.8 | loop fusion | flops 6291456 | bytes 25165824 | tf_op jit(solution)/shard_map/stack | solution.py:104
  264.6 5.2 %pad_maximum_fusion.1 = bf16[2,3072,1024]{2,1,0:T(8,128)(2,1)} fusion(bf16[1,3072,1024]{2,1,0:T(8,128)(2,1)S(1)} %convert_bitcast_fusion.2, bf16[1,3072,1024]{2,1,0:T(8,128)(2,1)S(1)} %convert_bitcast_fusion.3), kind=kLoop, calls=%fused_computation.7 | loop fusion | flops 6291456 | bytes 25165824 | tf_op jit(solution)/shard_map/stack | solution.py:103
  271.9 1.5 gather_fusion.4
  273.4 2.3 gather_fusion.5
  275.6 2.2 fusion.47
  277.9 5.4 %convert_bitcast_fusion.4 = bf16[1,3072,1024]{2,1,0:T(8,128)(2,1)S(1)} fusion(bf16[288,1024]{1,0:T(8,128)(2,1)S(1)} %copy-done.6, bf16[2,288,3072]{2,1,0:T(8,128)(2,1)} %all-gather.3.cloned.1.call-done), kind=kOutput, calls=%fused_computation.33 | convolution fusion | flops 1815085056 | bytes 8650752 | tf_op jit(solution)/shard_map/dot_general | solution.py:70
  283.3 5.2 %pad_maximum_fusion = bf16[2,3072,1024]{2,1,0:T(8,128)(2,1)} fusion(bf16[1,3072,1024]{2,1,0:T(8,128)(2,1)S(1)} %convert_bitcast_fusion.4, bf16[1,3072,1024]{2,1,0:T(8,128)(2,1)S(1)} %bitcast.124), kind=kLoop, calls=%fused_computation.6 | loop fusion | flops 6291456 | bytes 25165824 | tf_op jit(solution)/shard_map/stack | solution.py:102
  288.5 3.8 %reduce-scatter.9.cloned.1.call-done = bf16[128,1,1,768]{3,0,2,1:T(8,128)(2,1)} async-done(((bf16[128,2,1,768]{3,0,2,1:T(8,128)(2,1)}), bf16[128,1,1,768]{3,0,2,1:T(8,128)(2,1)}) %reduce-scatter.9.cloned.1.call-update) | async-done | bytes 196624 | tf_op jit(solution)/shard_map/reduce_scatter | solution.py:98
  (103 shorter events, 12.7 us)
Async XLA Ops:
  7.2 81.8 %all-gather.3.cloned.1.call-start = ((), (), s32[]{:S(2)}) async-start(), calls=%async_computation.3 | async-start | bytes 4423680 | tf_op jit(solution)/shard_map/all_gather | solution.py:42
  11.0 1.7 copy-start
  16.1 143.6 %all-gather.5.cloned.1.call-start = ((), (), s32[]{:S(2)}) async-start(), calls=%async_computation.4 | async-start | bytes 4423680 | tf_op jit(solution)/shard_map/all_gather | solution.py:43
  17.2 202.5 %reduce-scatter.7.cloned.1.call-start = ((), (), s32[]{:S(2)}) async-start(), calls=%async_computation.5 | async-start | bytes 5308416 | tf_op jit(solution)/shard_map/reduce_scatter | solution.py:90
  88.9 5.5 %copy-start.1 = (bf16[2,288,3072]{2,1,0:T(8,128)(2,1)S(1)}, bf16[2,288,3072]{2,1,0:T(8,128)(2,1)}, u32[]{:S(2)}) copy-start(bf16[2,288,3072]{2,1,0:T(8,128)(2,1)} %all-gather.3.cloned.1.call-done) | copy-start | bytes 10616836
  94.5 65.3 %copy-start.9 = (f32[288,1024]{1,0:T(8,128)}, f32[288,1024]{1,0:T(8,128)S(1)}, u32[]{:S(2)}) copy-start(f32[288,1024]{1,0:T(8,128)S(1)} %fusion.2) | copy-start | bytes 3538948
  100.2 65.2 %copy-start.11 = (f32[288,1024]{1,0:T(8,128)}, f32[288,1024]{1,0:T(8,128)S(1)}, u32[]{:S(2)}) copy-start(f32[288,1024]{1,0:T(8,128)S(1)} %fusion.6) | copy-start | bytes 3538948
  165.4 5.3 %copy-start.5 = (bf16[288,1024]{1,0:T(8,128)(2,1)}, bf16[288,1024]{1,0:T(8,128)(2,1)S(1)}, u32[]{:S(2)}) copy-start(bf16[288,1024]{1,0:T(8,128)(2,1)S(1)} %get-tuple-element.21) | copy-start | bytes 1769476
  165.4 5.3 %copy-start.14 = (bf16[288,1024]{1,0:T(8,128)(2,1)}, bf16[288,1024]{1,0:T(8,128)(2,1)S(1)}, u32[]{:S(2)}) copy-start(bf16[288,1024]{1,0:T(8,128)(2,1)S(1)} %get-tuple-element.20) | copy-start | bytes 1769476
  177.4 5.5 %copy-start.2 = (bf16[2,288,3072]{2,1,0:T(8,128)(2,1)S(1)}, bf16[2,288,3072]{2,1,0:T(8,128)(2,1)}, u32[]{:S(2)}) copy-start(bf16[2,288,3072]{2,1,0:T(8,128)(2,1)} %all-gather.3.cloned.1.call-done) | copy-start | bytes 10616836
  177.4 12.1 %slice-start.2 = ((s8[12582912]{0:T(1024)(128)(4,1)}), s8[4194304]{0:T(1024)(128)(4,1)S(1)}, s32[]{:S(2)}) async-start(s8[12582912]{0:T(1024)(128)(4,1)} %bitcast.125), calls=%async_computation.10 | async-start | bytes 8388608
  177.4 12.1 %slice-start.3 = ((s8[12582912]{0:T(1024)(128)(4,1)}), s8[4194304]{0:T(1024)(128)(4,1)S(1)}, s32[]{:S(2)}) async-start(s8[12582912]{0:T(1024)(128)(4,1)} %bitcast.125), calls=%async_computation.11 | async-start | bytes 8388608
  182.9 6.6 %copy-start.13 = (f32[288,1024]{1,0:T(8,128)}, f32[288,1024]{1,0:T(8,128)S(1)}, u32[]{:S(2)}) copy-start(f32[288,1024]{1,0:T(8,128)S(1)} %fusion.12) | copy-start | bytes 3538948
  182.9 6.6 %slice-start.4 = ((s8[12582912]{0:T(1024)(128)(4,1)}), s8[4194304]{0:T(1024)(128)(4,1)S(1)}, s32[]{:S(2)}) async-start(s8[12582912]{0:T(1024)(128)(4,1)} %bitcast.125), calls=%async_computation.12 | async-start | bytes 8388608
  182.9 11.6 %slice-start.5 = ((s8[12582912]{0:T(1024)(128)(4,1)}), s8[4194304]{0:T(1024)(128)(4,1)S(1)}, s32[]{:S(2)}) async-start(s8[12582912]{0:T(1024)(128)(4,1)} %bitcast.127), calls=%async_computation.13 | async-start | bytes 8388608
  183.0 11.6 %slice-start.6 = ((s8[12582912]{0:T(1024)(128)(4,1)}), s8[4194304]{0:T(1024)(128)(4,1)S(1)}, s32[]{:S(2)}) async-start(s8[12582912]{0:T(1024)(128)(4,1)} %bitcast.127), calls=%async_computation.14 | async-start | bytes 8388608
  189.5 5.1 %slice-start.7 = ((s8[12582912]{0:T(1024)(128)(4,1)}), s8[4194304]{0:T(1024)(128)(4,1)S(1)}, s32[]{:S(2)}) async-start(s8[12582912]{0:T(1024)(128)(4,1)} %bitcast.127), calls=%async_computation.15 | async-start | bytes 8388608
  194.6 2.1 copy-start.7
  194.6 2.1 copy-start.16
  209.6 60.2 %reduce-scatter.11.cloned.1.call-start = ((), (), s32[]{:S(2)}) async-start(), calls=%async_computation.7 | async-start | bytes 2211840
  223.0 12.5 %copy-start.17 = (bf16[288,1024]{1,0:T(8,128)(2,1)S(1)}, bf16[288,1024]{1,0:T(8,128)(2,1)}, u32[]{:S(2)}) copy-start(bf16[288,1024]{1,0:T(8,128)(2,1)} %get-tuple-element.18) | copy-start | bytes 1769476
  225.6 15.3 %copy-start.8 = (bf16[288,1024]{1,0:T(8,128)(2,1)S(1)}, bf16[288,1024]{1,0:T(8,128)(2,1)}, u32[]{:S(2)}) copy-start(bf16[288,1024]{1,0:T(8,128)(2,1)} %copy-done.7) | copy-start | bytes 1769476
  225.6 66.7 %reduce-scatter.9.cloned.1.call-start = ((), (), s32[]{:S(2)}) async-start(), calls=%async_computation.6 | async-start | bytes 589824 | tf_op jit(solution)/shard_map/reduce_scatter | solution.py:98
  235.5 5.4 %copy-start.3 = (bf16[2,288,3072]{2,1,0:T(8,128)(2,1)S(1)}, bf16[2,288,3072]{2,1,0:T(8,128)(2,1)}, u32[]{:S(2)}) copy-start(bf16[2,288,3072]{2,1,0:T(8,128)(2,1)} %all-gather.3.cloned.1.call-done) | copy-start | bytes 10616836
  240.9 5.4 %copy-start.15 = (bf16[288,1024]{1,0:T(8,128)(2,1)S(1)}, bf16[288,1024]{1,0:T(8,128)(2,1)}, u32[]{:S(2)}) copy-start(bf16[288,1024]{1,0:T(8,128)(2,1)} %copy-done.14) | copy-start | bytes 1769476
  246.3 3.7 %copy-start.4 = (bf16[2,288,3072]{2,1,0:T(8,128)(2,1)S(1)}, bf16[2,288,3072]{2,1,0:T(8,128)(2,1)}, u32[]{:S(2)}) copy-start(bf16[2,288,3072]{2,1,0:T(8,128)(2,1)} %all-gather.5.cloned.1.call-done) | copy-start | bytes 10616836
  246.3 3.8 %copy-start.10 = (f32[288,1024]{1,0:T(8,128)S(1)}, f32[288,1024]{1,0:T(8,128)}, u32[]{:S(2)}) copy-start(f32[288,1024]{1,0:T(8,128)} %copy-done.9) | copy-start | bytes 3538948
  246.3 3.8 %copy-start.12 = (f32[288,1024]{1,0:T(8,128)S(1)}, f32[288,1024]{1,0:T(8,128)}, u32[]{:S(2)}) copy-start(f32[288,1024]{1,0:T(8,128)} %copy-done.11) | copy-start | bytes 3538948
  271.8 6.1 %copy-start.6 = (bf16[288,1024]{1,0:T(8,128)(2,1)S(1)}, bf16[288,1024]{1,0:T(8,128)(2,1)}, u32[]{:S(2)}) copy-start(bf16[288,1024]{1,0:T(8,128)(2,1)} %copy-done.5) | copy-start | bytes 1769476
  275.6 7.6 %slice-start = ((s8[6291456]{0:T(1024)(128)(4,1)}), s8[2097152]{0:T(1024)(128)(4,1)S(1)}, s32[]{:S(2)}) async-start(s8[6291456]{0:T(1024)(128)(4,1)} %bitcast.123), calls=%async_computation.8 | async-start | bytes 4194304
  277.9 5.4 %slice-start.1 = ((s8[6291456]{0:T(1024)(128)(4,1)}), s8[4194304]{0:T(1024)(128)(4,1)S(1)}, s32[]{:S(2)}) async-start(s8[6291456]{0:T(1024)(128)(4,1)} %bitcast.123), calls=%async_computation.9 | async-start | bytes 8388608
Sparse Core Ops, SparseCore 0:
  16.3 72.6 all-gather.2
  91.1 68.5 all-gather.4
  209.7 10.0 reduce-scatter.6
  225.7 39.5 reduce-scatter.10
  278.0 14.2 reduce-scatter.8
where the time goes:
time: 305 us; the launch traced here: 299 us
  waiting for transfers between devices  145 us (48%)
  matrix products  81.1 us (27%)
  other arithmetic  25.3 us (8%)
  local copies, waits for them, and re-layouts  22.8 us (7%)
  between operations  14.6 us (5%)
  starting transfers between devices  10.1 us (3%)
    all_gather x1, waiting for transfers between devices, per_device(): lax.all_gather(local_tokens, 'ctx', axis=1, tiled=True)  71.7 us
    all_gather x1, waiting for transfers between devices, per_device(): lax.all_gather(local_grads, 'ctx', axis=1, tiled=True)  59.5 us
    dot_general x2, matrix products, per_device(): jnp.dot(rows_in, up_matrix[local], preferred_element_type=jnp.float32)  12.2 us
    dot_general x2, matrix products, per_device(): jnp.dot(up_part, up_matrix[partial_local].T, preferred_element_type=jnp.f...  11 us
    dot_general x2, matrix products, per_device(): jnp.dot(rows_in, gate_matrix[local], preferred_element_type=jnp.float32)  10.9 us
    dot_general x2, matrix products, per_device(): jnp.dot(rows_in.T, gate_grad, preferred_element_type=jnp.float32)  10.7 us
    dot_general x2, matrix products, per_device(): jnp.dot(grads_in, down_matrix[local].T, preferred_element_type=jnp.float32)  10.7 us
    reduce_scatter x1, waiting for transfers between devices, per_device(): lax.psum_scatter(complete.astype(jnp.bfloat16), 'tp', scatter_dimension=3...  10.1 us
  transfers between devices with their start and end apart: 5, of which 4 were waited for; matrix products, arithmetic and copies ran while one was open for 19% of the time, Pallas kernels for 0%

commit v1 on v0

v1 whole, which is shorter than its diff:
```python
import functools

import jax
import jax.numpy as jnp
from jax import lax
from jax.experimental import pallas as pl
from jax.experimental.pallas import tpu as pltpu
from jax.sharding import PartitionSpec as P

CAP = 72
VMEM_LIMIT = 56 * 1024 * 1024
F32 = jnp.float32
BF16 = jnp.bfloat16
NN = (((1,), (0,)), ((), ()))
NT = (((1,), (1,)), ((), ()))
TN = (((0,), (0,)), ((), ()))


def mm(a, b, dims):
    return lax.dot_general(a, b, dims, preferred_element_type=F32)


def params():
    return pltpu.CompilerParams(vmem_limit_bytes=VMEM_LIMIT)


def cost(flops, nbytes):
    return pl.CostEstimate(flops=int(flops), bytes_accessed=int(nbytes), transcendentals=0)


def whole(shape):
    return pl.BlockSpec(shape, lambda *_: (0,) * len(shape))


def shift(count, by):
    return [(i, (i + by) % count) for i in range(count)]


def pair_rows(metas, row, pair):
    first = metas[2 * pair][pl.ds(row, 1), :]
    second = metas[2 * pair + 1][pl.ds(row, 1), :]
    return first, second


def pair_one_hot(metas, expert, pair):
    first, second = pair_rows(metas, expert, pair)
    second = jnp.where(second >= 0, second + CAP, second)
    slot = jnp.concatenate([first, second], axis=1)
    rows = lax.broadcasted_iota(jnp.int32, (2 * CAP, slot.shape[1]), 0).astype(F32)
    return rows == slot


class Gathered:
    def __init__(self, refs, exp_count):
        self.own = refs[0]
        self.slabs = [(dx, dc, refs[1 + dx * 2 + dc]) for dx in range(exp_count) for dc in range(2)]

    def pack(self, here, exp_count, width, pair, hot, scale, store):
        for dx, dc, ref in self.slabs:
            x = lax.rem(here[0] + exp_count - dx, exp_count)
            c = lax.rem(here[1] + dc, 2)
            column = pl.multiple_of((x * 2 + c) * width, 128)
            if pair == 0:
                rows = jnp.concatenate([self.own[:, pl.ds(column, width)], ref[0]], axis=0)
            else:
                rows = jnp.concatenate([ref[2 * pair - 1], ref[2 * pair]], axis=0)
            packed = mm(hot, rows, NN)
            if scale is not None:
                packed = packed * scale
            store(column, packed.astype(BF16))


def forward_kernel(n, exp_count, width, here_ref, *refs):
    count = 1 + 2 * exp_count
    data = Gathered(refs[:count], exp_count)
    metas = refs[count:count + n]
    gate_w, up_w, xp_ref, hid_ref, act_ref, dact_ref = refs[count + n:]
    local = pl.program_id(0)
    here = (here_ref[0], here_ref[1])
    expert = here[0] * pl.num_programs(0) + local

    @pl.when(pl.program_id(1) == 0)
    def _():
        for pair in range(n // 2):
            hot = pair_one_hot(metas, expert, pair).astype(BF16)

            def store(column, value):
                xp_ref[local, pl.ds(pair * 2 * CAP, 2 * CAP), pl.ds(column, width)] = value

            data.pack(here, exp_count, width, pair, hot, None, store)

    rows = xp_ref[local]
    gate = mm(rows, gate_w[0], NN)
    up = mm(rows, up_w[0], NN)
    sig = jax.nn.sigmoid(gate)
    act = gate * sig
    hid_ref[0] = (act * up).astype(BF16)
    act_ref[0] = act
    dact_ref[0] = up * sig * (1.0 + gate * (1.0 - sig))


def hidden_kernel(n, exp_count, width, experts, here_ref, *refs):
    count = 1 + 2 * exp_count
    data = Gathered(refs[:count], exp_count)
    metas = refs[count:count + n]
    down_w, act_ref, dact_ref, gp_ref, gg_ref, ug_ref = refs[count + n:]
    local = pl.program_id(0)
    here = (here_ref[0], here_ref[1])
    expert = here[0] * pl.num_programs(0) + local

    @pl.when(pl.program_id(1) == 0)
    def _():
        for pair in range(n // 2):
            hot = pair_one_hot(metas, expert, pair)
            weights = jnp.concatenate(pair_rows(metas, experts + expert, pair), axis=1)
            scale = jnp.sum(jnp.where(hot, weights, 0.0), axis=1, keepdims=True)

            def store(column, value):
                gp_ref[local, pl.ds(pair * 2 * CAP, 2 * CAP), pl.ds(column, width)] = value

            data.pack(here, exp_count, width, pair, hot.astype(BF16), scale, store)

    hidden_grad = mm(gp_ref[local], down_w[0], NT)
    ug_ref[0] = (hidden_grad * act_ref[0]).astype(BF16)
    gg_ref[0] = (hidden_grad * dact_ref[0]).astype(BF16)


def rows_kernel(n, local_count, has_add, pick_ref, here_ref, *refs):
    del pick_ref
    metas = refs[:n]
    gg_ref, ug_ref, gate_w, up_w = refs[n:n + 4]
    add_ref = refs[n + 4] if has_add else None
    out_ref = refs[-1]
    terms = []
    for local in range(local_count):
        expert = here_ref[0] * local_count + local
        term = mm(gg_ref[local], gate_w[local], NT) + mm(ug_ref[local], up_w[local], NT)
        terms.append((expert, term.astype(BF16)))
    for pair in range(n // 2):
        total = None
        for expert, term in terms:
            hot = pair_one_hot(metas, expert, pair).astype(BF16)
            part = mm(hot, term[pair * 2 * CAP:(pair + 1) * 2 * CAP], TN)
            total = part if total is None else total + part
        half = total.shape[0] // 2
        for k in range(2):
            block = total[k * half:(k + 1) * half]
            if has_add:
                block = block + add_ref[2 * pair + k].astype(F32)
            out_ref[2 * pair + k] = block.astype(BF16)


def outer_kernel(a_ref, b_ref, out_ref):
    out_ref[0] = mm(a_ref[0], b_ref[0], TN).astype(BF16)


def weight_grad(a, b):
    experts, slots, m = a.shape
    cols = b.shape[2]
    tile = min(512, m)
    return pl.pallas_call(
        outer_kernel,
        out_shape=jax.ShapeDtypeStruct((experts, m, cols), BF16),
        grid=(experts, m // tile),
        in_specs=[
            pl.BlockSpec((1, slots, tile), lambda e, i: (e, 0, i)),
            pl.BlockSpec((1, slots, cols), lambda e, i: (e, 0, 0)),
        ],
        out_specs=pl.BlockSpec((1, tile, cols), lambda e, i: (e, i, 0)),
        compiler_params=params(),
        cost_estimate=cost(2 * a.size * cols, 2 * (a.size + b.size + experts * m * cols)),
    )(a, b)


def gather_blocks(mine, n, exp_count):
    others = jnp.stack([lax.ppermute(mine, "ctx", shift(n, s)) for s in range(1, n)])
    slabs = []
    for dx in range(exp_count):
        part = others if dx == 0 else lax.ppermute(others, "exp", shift(exp_count, dx))
        slabs += [part, lax.ppermute(part, "tp", shift(2, 1))]
    return slabs


def per_device(tokens, out_grad, expert_ids, gate_weights, gate_matrix, up_matrix, down_matrix):
    n = lax.axis_size("ctx")
    exp_count = lax.axis_size("exp")
    x = lax.axis_index("exp")
    c = lax.axis_index("tp")
    local_count, depth, hidden_units = gate_matrix.shape
    experts = local_count * exp_count
    block, _ = tokens.shape
    width = depth // (exp_count * 2)
    slots = n * CAP
    here = jnp.stack([x, c]).astype(jnp.int32)
    column = (x * 2 + c) * width

    names = jnp.arange(experts, dtype=jnp.int32)[:, None]
    chosen = [expert_ids[:, k][None, :] == names for k in range(expert_ids.shape[1])]
    member = functools.reduce(jnp.logical_or, chosen)
    before = jnp.arange(block)[:, None] <= jnp.arange(block)[None, :]
    order = jnp.dot(member.astype(BF16), before.astype(BF16), preferred_element_type=F32)
    slot = jnp.where(member, order - 1.0, -1.0)
    weight = sum(jnp.where(ch, gate_weights[:, k][None, :], 0.0) for k, ch in enumerate(chosen))
    meta = jnp.concatenate([slot, weight], axis=0)

    token_part = lax.dynamic_slice_in_dim(tokens, column, width, axis=1)
    grad_part = lax.dynamic_slice_in_dim(out_grad, column, width, axis=1)
    token_slabs = gather_blocks(token_part, n, exp_count)
    metas = [meta] + [lax.ppermute(meta, "ctx", shift(n, s)) for s in range(1, n)]
    grad_slabs = gather_blocks(grad_part, n, exp_count)

    slab_specs = [whole((block, depth))] + [whole((n - 1, block, width))] * (2 * exp_count)
    meta_specs = [whole(meta.shape)] * n
    tile = min(256, hidden_units)
    grid = (local_count, hidden_units // tile)
    packed = jax.ShapeDtypeStruct((local_count, slots, depth), BF16)
    packed_spec = pl.BlockSpec((local_count, slots, depth), lambda *_: (0, 0, 0))
    units = lambda dtype: jax.ShapeDtypeStruct((local_count, slots, hidden_units), dtype)
    units_spec = pl.BlockSpec((1, slots, tile), lambda e, j, *_: (e, 0, j))
    flops = 2 * local_count * slots * depth * hidden_units
    weight_bytes = 2 * gate_matrix.size

    xp, hidden, act, dact = pl.pallas_call(
        functools.partial(forward_kernel, n, exp_count, width),
        out_shape=(packed, units(BF16), units(F32), units(F32)),
        grid_spec=pltpu.PrefetchScalarGridSpec(
            num_scalar_prefetch=1,
            grid=grid,
            in_specs=slab_specs + meta_specs
            + [pl.BlockSpec((1, depth, tile), lambda e, j, *_: (e, 0, j))] * 2,
            out_specs=(packed_spec, units_spec, units_spec, units_spec),
        ),
        compiler_params=params(),
        cost_estimate=cost(2 * flops, 2 * weight_bytes),
    )(here, tokens, *token_slabs, *metas, gate_matrix, up_matrix)

    gp, gate_grad, up_grad = pl.pallas_call(
        functools.partial(hidden_kernel, n, exp_count, width, experts),
        out_shape=(packed, units(BF16), units(BF16)),
        grid_spec=pltpu.PrefetchScalarGridSpec(
            num_scalar_prefetch=1,
            grid=grid,
            in_specs=slab_specs + meta_specs
            + [pl.BlockSpec((1, tile, depth), lambda e, j, *_: (e, j, 0)), units_spec, units_spec],
            out_specs=(packed_spec, units_spec, units_spec),
        ),
        compiler_params=params(),
        cost_estimate=cost(flops, weight_bytes),
    )(here, out_grad, *grad_slabs, *metas, down_matrix, act, dact)

    def row_grads(slab, add):
        part_spec = pl.BlockSpec((local_count, width, hidden_units), lambda i, pick, *_: (0, pick[0], 0))
        adds = [] if add is None else [add]
        return pl.pallas_call(
            functools.partial(rows_kernel, n, local_count, add is not None),
            out_shape=jax.ShapeDtypeStruct((n, block, width), BF16),
            grid_spec=pltpu.PrefetchScalarGridSpec(
                num_scalar_prefetch=2,
                grid=(1,),
                in_specs=meta_specs
                + [whole((local_count, slots, hidden_units))] * 2
                + [part_spec] * 2
                + [whole((n, block, width))] * len(adds),
                out_specs=whole((n, block, width)),
            ),
            compiler_params=params(),
            cost_estimate=cost(2 * flops * width // depth, 2 * weight_bytes * width // depth),
        )(slab.reshape(1).astype(jnp.int32), here, *metas, gate_grad, up_grad, gate_matrix, up_matrix, *adds)

    def slab_of(dx, dc):
        return lax.rem(x + dx, exp_count) * 2 + lax.rem(c + dc, 2)

    order_dx = list(range(1, exp_count)) + [0]
    siblings = [lax.ppermute(row_grads(slab_of(dx, 1), None), "tp", shift(2, 1)) for dx in order_dx]
    received = []
    for dx, sibling in zip(order_dx, siblings):
        own = row_grads(slab_of(dx, 0), sibling)
        if dx:
            received.append(lax.ppermute(own, "exp", shift(exp_count, dx)))
    total = own.astype(F32)
    for part in received:
        total = total + part.astype(F32)
    rounded = total.astype(BF16)
    final = total[0]
    for s in range(1, n):
        final = final + lax.ppermute(rounded[s], "ctx", shift(n, -s)).astype(F32)
    grad_tokens = final.astype(BF16)

    grad_down = weight_grad(hidden, gp)
    grad_gate = weight_grad(xp, gate_grad)
    grad_up = weight_grad(xp, up_grad)
    return (grad_gate, grad_up, grad_down, grad_tokens)


def solution(mesh):
    in_specs = (
        P(("groups", "ctx"), None),
        P(("groups", "ctx"), None),
        P(("groups", "ctx"), None),
        P(("groups", "ctx"), None),
        P("exp", None, ("ctx", "tp")),
        P("exp", None, ("ctx", "tp")),
        P("exp", ("ctx", "tp"), None),
    )
    out_specs = (
        P(("groups", "exp"), None, ("ctx", "tp")),
        P(("groups", "exp"), None, ("ctx", "tp")),
        P(("groups", "exp"), ("ctx", "tp"), None),
        P(("groups", "ctx"), ("exp", "tp")),
    )
    return jax.shard_map(
        per_device, mesh=mesh, in_specs=in_specs, out_specs=out_specs, check_vma=False
    )
```

time: 305 us -> 181 us (0.59); the launches traced: 299 us -> 180 us
  Pallas kernels: 0 us -> 105 us
  waiting for transfers between devices: 145 us -> 45.8 us
  matrix products: 81.1 us -> 0.14 us
  other arithmetic: 25.3 us -> 2.9 us
  local copies, waits for them, and re-layouts: 22.8 us -> 7.11 us
  between operations: 14.6 us -> 0.91 us
  starting transfers between devices: 10.1 us -> 18.4 us
    all_gather x2 -> x0, waiting for transfers between devices: 131 us -> none  [the longest x1 71.7 us: per_device(): lax.all_gather(local_tokens, 'ctx', axis=1, tiled=True)]
    pallas_call x0 -> x9, Pallas kernels: none -> 105 us  [the longest x3 39.2 us: weight_grad(): pl.pallas_call(outer_kernel, out_shape=jax.ShapeDtypeStruct((experts, m,...]
    dot_general x16 -> x1, matrix products: 81.1 us -> 0.14 us  [per_device(): jnp.dot(member.astype(BF16), before.astype(BF16), preferred_element_type=...]
    ppermute x0 -> x21, waiting for transfers between devices: none -> 45.8 us  [the longest x6 29.4 us: gather_blocks(): lax.ppermute(mine, 'ctx', shift(n, s))]
    another operation x10 -> x3, other arithmetic: 20.4 us -> 0.78 us  [the longest x1 0.65 us: per_device(): here = jnp.stack([x, c]).astype(jnp.int32)]
    ppermute x0 -> x21, starting transfers between devices: none -> 18.4 us  [the longest x6 11 us: gather_blocks(): lax.ppermute(mine, 'ctx', shift(n, s))]
    reduce_scatter x2 -> x0, waiting for transfers between devices: 13.8 us -> none  [the longest x1 10.1 us: per_device(): lax.psum_scatter(complete.astype(jnp.bfloat16), 'tp', scatter_dimension=3...]
    reduce_scatter x2 -> x0, starting transfers between devices: 9.96 us -> none  [the longest x1 9.92 us: per_device(): lax.psum_scatter(summed.astype(jnp.bfloat16), 'exp', scatter_dimension=1,...]
  transfers between devices with their start and end apart: 5 -> 21, of which waited for: 4 -> 8; matrix products, arithmetic and copies ran while one was open for 19% -> 1% of each run, Pallas kernels for 0% -> 46%
where the time goes in v1:
time: 181 us; the launch traced here: 180 us
  Pallas kernels  105 us (58%)
  waiting for transfers between devices  45.8 us (25%)
  starting transfers between devices  18.4 us (10%)
  local copies, waits for them, and re-layouts  7.11 us (4%)
  other arithmetic  2.9 us (2%)
    pallas_call x3, Pallas kernels, weight_grad(): pl.pallas_call(outer_kernel, out_shape=jax.ShapeDtypeStruct((experts, m,...  39.2 us
    pallas_call x4, Pallas kernels, row_grads(): pl.pallas_call(functools.partial(rows_kernel, n, local_count, add is not...  31 us
    ppermute x6, waiting for transfers between devices, gather_blocks(): lax.ppermute(mine, 'ctx', shift(n, s))  29.4 us
    pallas_call x1, Pallas kernels, per_device(): pl.pallas_call(functools.partial(forward_kernel, n, exp_count, width), ou...  19.2 us
    pallas_call x1, Pallas kernels, per_device(): pl.pallas_call(functools.partial(hidden_kernel, n, exp_count, width, expe...  15 us
    ppermute x6, starting transfers between devices, gather_blocks(): lax.ppermute(mine, 'ctx', shift(n, s))  11 us
    ppermute x2, waiting for transfers between devices, gather_blocks(): lax.ppermute(others, 'exp', shift(exp_count, dx))  8.29 us
    unnamed x30, local copies, waits for them, and re-layouts  4.42 us
  transfers between devices with their start and end apart: 21, of which 8 were waited for; matrix products, arithmetic and copies ran while one was open for 1% of the time, Pallas kernels for 46%

profile of v1, /device:TPU:0, one launch (start us, length us, event | category | flops | bytes accessed | tf_op | source)
XLA Modules:
  0.0 179.8 jit_solution(971683459762824952)
XLA Ops:
  0.7 0.9 constant_dynamic-slice_fusion.1
  1.6 5.1 %collective-permute-start.2 = (bf16[128,768]{1,0:T(8,128)(2,1)S(1)}, bf16[128,768]{1,0:T(8,128)(2,1)S(1)}, u32[]{:S(2)}, u32[]{:S(2)}) collective-permute-start(bf16[128,768]{1,0:T(8,128)(2,1)S(1)} %constant_dynamic-slice_fusion.1), channel_id=1, source_target_pairs={{0,12},{4,0},{8,4},{12,8},{1,13},{5,1},{9,5},{13,9},{2,14},{6,2},{... | collective-permute-start | bytes 589832 | tf_op jit(solution)/shard_map/ppermute | solution.py:176
  6.7 1.0 collective-permute-start
  7.7 4.3 %collective-permute-done.2 = bf16[128,768]{1,0:T(8,128)(2,1)S(1)} collective-permute-done((bf16[128,768]{1,0:T(8,128)(2,1)S(1)}, bf16[128,768]{1,0:T(8,128)(2,1)S(1)}, u32[]{:S(2)}, u32[]{:S(2)}) %collective-permute-start.2) | collective-permute-done | bytes 196640 | tf_op jit(solution)/shard_map/ppermute | solution.py:176
  12.1 11.3 %collective-permute-done.1 = bf16[128,768]{1,0:T(8,128)(2,1)S(1)} collective-permute-done((bf16[128,768]{1,0:T(8,128)(2,1)S(1)}, bf16[128,768]{1,0:T(8,128)(2,1)S(1)}, u32[]{:S(2)}, u32[]{:S(2)}) %collective-permute-start.1) | collective-permute-done | bytes 196640 | tf_op jit(solution)/shard_map/ppermute | solution.py:176
  23.5 1.6 collective-permute-start.4
  25.0 0.9 constant_dynamic-slice_fusion
  26.4 2.5 %collective-permute-start.10 = (bf16[128,768]{1,0:T(8,128)(2,1)S(1)}, bf16[128,768]{1,0:T(8,128)(2,1)S(1)}, u32[]{:S(2)}, u32[]{:S(2)}) collective-permute-start(bf16[128,768]{1,0:T(8,128)(2,1)S(1)} %constant_dynamic-slice_fusion), channel_id=1, source_target_pairs={{0,8},{4,12},{8,0},{12,4},{1,9},{5,13},{9,1},{13,5},{2,10},{6,14},... | collective-permute-start | bytes 589832 | tf_op jit(solution)/shard_map/ppermute | solution.py:176
  28.9 1.9 %collective-permute-start.9 = (bf16[128,768]{1,0:T(8,128)(2,1)S(1)}, bf16[128,768]{1,0:T(8,128)(2,1)S(1)}, u32[]{:S(2)}, u32[]{:S(2)}) collective-permute-start(bf16[128,768]{1,0:T(8,128)(2,1)S(1)} %constant_dynamic-slice_fusion), channel_id=1, source_target_pairs={{0,4},{4,8},{8,12},{12,0},{1,5},{5,9},{9,13},{13,1},{2,6},{6,10},{... | collective-permute-start | bytes 589832 | tf_op jit(solution)/shard_map/ppermute | solution.py:176
  30.9 0.8 slice_bitcast_fusion.7
  32.3 13.2 %collective-permute-done.10 = bf16[128,768]{1,0:T(8,128)(2,1)S(1)} collective-permute-done((bf16[128,768]{1,0:T(8,128)(2,1)S(1)}, bf16[128,768]{1,0:T(8,128)(2,1)S(1)}, u32[]{:S(2)}, u32[]{:S(2)}) %collective-permute-start.10) | collective-permute-done | bytes 196640 | tf_op jit(solution)/shard_map/ppermute | solution.py:176
  46.5 3.4 %collective-permute-done.8.refs_8_.refs_3_ = f32[8,128]{1,0:T(8,128)S(1)} collective-permute-done((f32[8,128]{1,0:T(8,128)S(1)}, f32[8,128]{1,0:T(8,128)S(1)}, u32[]{:S(2)}, u32[]{:S(2)}) %collective-permute-start.8) | collective-permute-done | bytes 4128 | tf_op jit(solution)/shard_map/ppermute | solution.py:209
  49.9 0.6 pad_add_fusion.here_ref
  50.9 8.3 %collective-permute-done.13.refs_3_ = bf16[3,128,768]{2,1,0:T(8,128)(2,1)S(1)} collective-permute-done((bf16[3,128,768]{2,1,0:T(8,128)(2,1)S(1)}, bf16[3,128,768]{2,1,0:T(8,128)(2,1)S(1)}, u32[]{:S(2)}, u32[]{:S(2)}) %collective-permute-start.13) | collective-permute-done | bytes 589856 | tf_op jit(solution)/shard_map/ppermute | solution.py:179
  60.1 0.8 copy-done.6
  60.9 19.2 %shard_map.102 = (bf16[2,288,3072]{2,1,0:T(8,128)(2,1)}, bf16[2,288,1024]{2,1,0:T(8,128)(2,1)}, f32[2,288,1024]{2,1,0:T(8,128)}, f32[2,288,1024]{2,1,0:T(8,128)}) custom-call(s32[2]{0:T(128)} %pad_add_fusion.here_ref, bf16[128,3072]{1,0:T(8,128)(2,1)} %refs_0_.2, bf16[3,128,768]{2,1,0:T(8,128)(2,1)} %copy-done, bf16[3,128,768]{2,1,0:T(8,128)(2,1)} %copy-done.5, ...), custom_call_target="tpu_custom_call" | custom-call | flops 7247757312 | bytes 25165824 | tf_op jit(solution)/shard_map/pallas_call | solution.py:223
  80.2 0.8 copy-done.8
  81.2 15.0 %shard_map.103 = (bf16[2,288,3072]{2,1,0:T(8,128)(2,1)}, bf16[2,288,1024]{2,1,0:T(8,128)(2,1)}, bf16[2,288,1024]{2,1,0:T(8,128)(2,1)}) custom-call(s32[2]{0:T(128)} %pad_add_fusion.here_ref, bf16[128,3072]{1,0:T(8,128)(2,1)} %refs_0_.3, bf16[3,128,768]{2,1,0:T(8,128)(2,1)} %copy-done.1, bf16[3,128,768]{2,1,0:T(8,128)(2,1)} %copy-done.8, ...), custom_call_target="tpu_custom_call" | custom-call | flops 3623878656 | bytes 12582912 | tf_op jit(solution)/shard_map/pallas_call | solution.py:237
  96.2 7.6 %shard_map.109 = bf16[4,128,768]{2,1,0:T(8,128)(2,1)} custom-call(s32[1]{0:T(128)} %bitcast.15.pick_ref, s32[2]{0:T(128)} %pad_add_fusion.here_ref, f32[8,128]{1,0:T(8,128)} %copy-done.10, f32[8,128]{1,0:T(8,128)} %copy-done.13, f32[8,128]{1,0:T(8,128)} %copy-done.12, f32[8,128]{1,0:T(8,128)} %copy-done.11, ...), custom_call_target="tpu_custom_call" | custom-call | flops 1811939328 | bytes 6291456 | tf_op jit(solution)/shard_map/pallas_call | solution.py:254
  104.3 7.7 %shard_map.107 = bf16[4,128,768]{2,1,0:T(8,128)(2,1)} custom-call(s32[1]{0:T(128)} %bitcast.13.pick_ref, s32[2]{0:T(128)} %pad_add_fusion.here_ref, f32[8,128]{1,0:T(8,128)} %copy-done.10, f32[8,128]{1,0:T(8,128)} %copy-done.13, f32[8,128]{1,0:T(8,128)} %copy-done.12, f32[8,128]{1,0:T(8,128)} %copy-done.11, ...), custom_call_target="tpu_custom_call" | custom-call | flops 1811939328 | bytes 6291456 | tf_op jit(solution)/shard_map/pallas_call | solution.py:254
  112.1 0.9 copy-done.2
  113.0 7.8 %shard_map.110 = bf16[4,128,768]{2,1,0:T(8,128)(2,1)} custom-call(s32[1]{0:T(128)} %bitcast.14.pick_ref, s32[2]{0:T(128)} %pad_add_fusion.here_ref, f32[8,128]{1,0:T(8,128)} %copy-done.10, f32[8,128]{1,0:T(8,128)} %copy-done.13, f32[8,128]{1,0:T(8,128)} %copy-done.12, f32[8,128]{1,0:T(8,128)} %copy-done.11, ...), custom_call_target="tpu_custom_call" | custom-call | flops 1811939328 | bytes 6291456 | tf_op jit(solution)/shard_map/pallas_call | solution.py:254
  121.4 13.9 %shard_map.105 = bf16[2,3072,1024]{2,1,0:T(8,128)(2,1)} custom-call(bf16[2,288,3072]{2,1,0:T(8,128)(2,1)} %get-tuple-element.11.a_ref, bf16[2,288,1024]{2,1,0:T(8,128)(2,1)} %get-tuple-element.15.b_ref.refs_5_), custom_call_target="tpu_custom_call" | custom-call | flops 3623878656 | bytes 17301504 | tf_op jit(solution)/shard_map/pallas_call | solution.py:161
  135.3 13.9 %shard_map.104 = bf16[2,3072,1024]{2,1,0:T(8,128)(2,1)} custom-call(bf16[2,288,3072]{2,1,0:T(8,128)(2,1)} %get-tuple-element.11.a_ref, bf16[2,288,1024]{2,1,0:T(8,128)(2,1)} %get-tuple-element.14.b_ref.refs_4_), custom_call_target="tpu_custom_call" | custom-call | flops 3623878656 | bytes 17301504 | tf_op jit(solution)/shard_map/pallas_call | solution.py:161
  149.2 0.9 copy-done.3
  150.0 7.9 %shard_map.108 = bf16[4,128,768]{2,1,0:T(8,128)(2,1)} custom-call(s32[1]{0:T(128)} %bitcast.12.pick_ref, s32[2]{0:T(128)} %pad_add_fusion.here_ref, f32[8,128]{1,0:T(8,128)} %copy-done.10, f32[8,128]{1,0:T(8,128)} %copy-done.13, f32[8,128]{1,0:T(8,128)} %copy-done.12, f32[8,128]{1,0:T(8,128)} %copy-done.11, ...), custom_call_target="tpu_custom_call" | custom-call | flops 1811939328 | bytes 6291456 | tf_op jit(solution)/shard_map/pallas_call | solution.py:254
  157.9 1.3 fusion.9
  159.4 2.0 %collective-permute-start.20 = (bf16[128,768]{1,0:T(8,128)(2,1)S(1)}, bf16[128,768]{1,0:T(8,128)(2,1)S(1)}, u32[]{:S(2)}, u32[]{:S(2)}) collective-permute-start(bf16[128,768]{1,0:T(8,128)(2,1)S(1)} %get-tuple-element.21), channel_id=1, source_target_pairs={{0,4},{4,8},{8,12},{12,0},{1,5},{5,9},{9,13},{13,1},{2,6},{6,10},{... | collective-permute-start | bytes 589832 | tf_op jit(solution)/shard_map/ppermute | solution.py:286
  161.4 1.8 %collective-permute-start.19 = (bf16[128,768]{1,0:T(8,128)(2,1)S(1)}, bf16[128,768]{1,0:T(8,128)(2,1)S(1)}, u32[]{:S(2)}, u32[]{:S(2)}) collective-permute-start(bf16[128,768]{1,0:T(8,128)(2,1)S(1)} %get-tuple-element.22), channel_id=1, source_target_pairs={{0,8},{4,12},{8,0},{12,4},{1,9},{5,13},{9,1},{13,5},{2,10},{6,14},... | collective-permute-start | bytes 589832 | tf_op jit(solution)/shard_map/ppermute | solution.py:286
  163.2 11.5 %shard_map.106 = bf16[2,1024,3072]{2,1,0:T(8,128)(2,1)} custom-call(bf16[2,288,1024]{2,1,0:T(8,128)(2,1)} %get-tuple-element.16.a_ref, bf16[2,288,3072]{2,1,0:T(8,128)(2,1)} %get-tuple-element.17.b_ref), custom_call_target="tpu_custom_call" | custom-call | flops 3623878656 | bytes 17301504 | tf_op jit(solution)/shard_map/pallas_call | solution.py:161
  174.7 4.3 %collective-permute-done.19 = bf16[128,768]{1,0:T(8,128)(2,1)S(1)} collective-permute-done((bf16[128,768]{1,0:T(8,128)(2,1)S(1)}, bf16[128,768]{1,0:T(8,128)(2,1)S(1)}, u32[]{:S(2)}, u32[]{:S(2)}) %collective-permute-start.19) | collective-permute-done | bytes 196640 | tf_op jit(solution)/shard_map/ppermute | solution.py:286
  179.0 0.8 fusion.4
  (62 shorter events, 4.6 us)
Async XLA Ops:
  0.6 45.6 %copy-start.14 = (f32[128,2]{0,1:T(2,128)S(1)}, f32[128,2]{0,1:T(2,128)}, u32[]{:S(2)}) copy-start(f32[128,2]{0,1:T(2,128)} %param.10) | copy-start | bytes 3076
  1.6 10.5 %collective-permute-start.2 = (bf16[128,768]{1,0:T(8,128)(2,1)S(1)}, bf16[128,768]{1,0:T(8,128)(2,1)S(1)}, u32[]{:S(2)}, u32[]{:S(2)}) collective-permute-start(bf16[128,768]{1,0:T(8,128)(2,1)S(1)} %constant_dynamic-slice_fusion.1), channel_id=1, source_target_pairs={{0,12},{4,0},{8,4},{12,8},{1,13},{5,1},{9,5},{13,9},{2,14},{6,2},{... | collective-permute-start | bytes 589832 | tf_op jit(solution)/shard_map/ppermute | solution.py:176
  6.7 16.7 %collective-permute-start.1 = (bf16[128,768]{1,0:T(8,128)(2,1)S(1)}, bf16[128,768]{1,0:T(8,128)(2,1)S(1)}, u32[]{:S(2)}, u32[]{:S(2)}) collective-permute-start(bf16[128,768]{1,0:T(8,128)(2,1)S(1)} %constant_dynamic-slice_fusion.1), channel_id=1, source_target_pairs={{0,8},{4,12},{8,0},{12,4},{1,9},{5,13},{9,1},{13,5},{2,10},{6,14},... | collective-permute-start | bytes 589832 | tf_op jit(solution)/shard_map/ppermute | solution.py:176
  6.7 16.7 %collective-permute-start = (bf16[128,768]{1,0:T(8,128)(2,1)S(1)}, bf16[128,768]{1,0:T(8,128)(2,1)S(1)}, u32[]{:S(2)}, u32[]{:S(2)}) collective-permute-start(bf16[128,768]{1,0:T(8,128)(2,1)S(1)} %constant_dynamic-slice_fusion.1), channel_id=1, source_target_pairs={{0,4},{4,8},{8,12},{12,0},{1,5},{5,9},{9,13},{13,1},{2,6},{6,10},{... | collective-permute-start | bytes 589832 | tf_op jit(solution)/shard_map/ppermute | solution.py:176
  23.5 35.8 %copy-start = (bf16[3,128,768]{2,1,0:T(8,128)(2,1)}, bf16[3,128,768]{2,1,0:T(8,128)(2,1)S(1)}, u32[]{:S(2)}) copy-start(bf16[3,128,768]{2,1,0:T(8,128)(2,1)S(1)} %pad_maximum_fusion.refs_1_) | copy-start | bytes 1769476
  23.5 22.7 %collective-permute-start.4 = (bf16[3,128,768]{2,1,0:T(8,128)(2,1)S(1)}, bf16[3,128,768]{2,1,0:T(8,128)(2,1)S(1)}, u32[]{:S(2)}, u32[]{:S(2)}) collective-permute-start(bf16[3,128,768]{2,1,0:T(8,128)(2,1)S(1)} %pad_maximum_fusion.refs_1_), channel_id=1, source_target_pairs={{0,2},{2,0},{1,3},{3,1},{4,6},{6,4},{5,7},{7,5},{8,10},{10,8},{9,1... | collective-permute-start | bytes 1769480 | tf_op jit(solution)/shard_map/ppermute | solution.py:179
  26.0 6.3 %collective-permute-start.11 = (bf16[128,768]{1,0:T(8,128)(2,1)S(1)}, bf16[128,768]{1,0:T(8,128)(2,1)S(1)}, u32[]{:S(2)}, u32[]{:S(2)}) collective-permute-start(bf16[128,768]{1,0:T(8,128)(2,1)S(1)} %constant_dynamic-slice_fusion), channel_id=1, source_target_pairs={{0,12},{4,0},{8,4},{12,8},{1,13},{5,1},{9,5},{13,9},{2,14},{6,2},{... | collective-permute-start | bytes 589832 | tf_op jit(solution)/shard_map/ppermute | solution.py:176
  26.4 19.1 %collective-permute-start.10 = (bf16[128,768]{1,0:T(8,128)(2,1)S(1)}, bf16[128,768]{1,0:T(8,128)(2,1)S(1)}, u32[]{:S(2)}, u32[]{:S(2)}) collective-permute-start(bf16[128,768]{1,0:T(8,128)(2,1)S(1)} %constant_dynamic-slice_fusion), channel_id=1, source_target_pairs={{0,8},{4,12},{8,0},{12,4},{1,9},{5,13},{9,1},{13,5},{2,10},{6,14},... | collective-permute-start | bytes 589832 | tf_op jit(solution)/shard_map/ppermute | solution.py:176
  28.9 16.6 %collective-permute-start.9 = (bf16[128,768]{1,0:T(8,128)(2,1)S(1)}, bf16[128,768]{1,0:T(8,128)(2,1)S(1)}, u32[]{:S(2)}, u32[]{:S(2)}) collective-permute-start(bf16[128,768]{1,0:T(8,128)(2,1)S(1)} %constant_dynamic-slice_fusion), channel_id=1, source_target_pairs={{0,4},{4,8},{8,12},{12,0},{1,5},{5,9},{9,13},{13,1},{2,6},{6,10},{... | collective-permute-start | bytes 589832 | tf_op jit(solution)/shard_map/ppermute | solution.py:176
  31.8 27.5 %collective-permute-start.3 = (bf16[3,128,768]{2,1,0:T(8,128)(2,1)S(1)}, bf16[3,128,768]{2,1,0:T(8,128)(2,1)S(1)}, u32[]{:S(2)}, u32[]{:S(2)}) collective-permute-start(bf16[3,128,768]{2,1,0:T(8,128)(2,1)S(1)} %pad_maximum_fusion.refs_1_), channel_id=1, source_target_pairs={{0,1},{1,0},{2,3},{3,2},{4,5},{5,4},{6,7},{7,6},{8,9},{9,8},{10,11... | collective-permute-start | bytes 1769480 | tf_op jit(solution)/shard_map/ppermute | solution.py:180
  45.6 34.5 %copy-start.1 = (bf16[3,128,768]{2,1,0:T(8,128)(2,1)}, bf16[3,128,768]{2,1,0:T(8,128)(2,1)S(1)}, u32[]{:S(2)}) copy-start(bf16[3,128,768]{2,1,0:T(8,128)(2,1)S(1)} %pad_maximum_fusion.1.refs_1_) | copy-start | bytes 1769476
  45.6 13.6 %collective-permute-start.13 = (bf16[3,128,768]{2,1,0:T(8,128)(2,1)S(1)}, bf16[3,128,768]{2,1,0:T(8,128)(2,1)S(1)}, u32[]{:S(2)}, u32[]{:S(2)}) collective-permute-start(bf16[3,128,768]{2,1,0:T(8,128)(2,1)S(1)} %pad_maximum_fusion.1.refs_1_), channel_id=1, source_target_pairs={{0,2},{2,0},{1,3},{3,1},{4,6},{6,4},{5,7},{7,5},{8,10},{10,8},{9,1... | collective-permute-start | bytes 1769480 | tf_op jit(solution)/shard_map/ppermute | solution.py:179
  46.2 13.1 %copy-start.4 = (bf16[3,128,768]{2,1,0:T(8,128)(2,1)}, bf16[3,128,768]{2,1,0:T(8,128)(2,1)S(1)}, u32[]{:S(2)}) copy-start(bf16[3,128,768]{2,1,0:T(8,128)(2,1)S(1)} %collective-permute-done.4.refs_3_) | copy-start | bytes 1769476
  46.2 13.0 %collective-permute-start.5 = (bf16[3,128,768]{2,1,0:T(8,128)(2,1)S(1)}, bf16[3,128,768]{2,1,0:T(8,128)(2,1)S(1)}, u32[]{:S(2)}, u32[]{:S(2)}) collective-permute-start(bf16[3,128,768]{2,1,0:T(8,128)(2,1)S(1)} %collective-permute-done.4.refs_3_), channel_id=1, source_target_pairs={{0,1},{1,0},{2,3},{3,2},{4,5},{5,4},{6,7},{7,6},{8,9},{9,8},{10,11... | collective-permute-start | bytes 1769480 | tf_op jit(solution)/shard_map/ppermute | solution.py:180
  46.2 13.0 %copy-start.10 = (f32[8,128]{1,0:T(8,128)}, f32[8,128]{1,0:T(8,128)S(1)}, u32[]{:S(2)}) copy-start(f32[8,128]{1,0:T(8,128)S(1)} %pad_maximum_fusion.2.refs_5_.refs_0_) | copy-start | bytes 12292
  46.2 3.7 %collective-permute-start.8 = (f32[8,128]{1,0:T(8,128)S(1)}, f32[8,128]{1,0:T(8,128)S(1)}, u32[]{:S(2)}, u32[]{:S(2)}) collective-permute-start(f32[8,128]{1,0:T(8,128)S(1)} %pad_maximum_fusion.2.refs_5_.refs_0_), channel_id=1, source_target_pairs={{0,12},{4,0},{8,4},{12,8},{1,13},{5,1},{9,5},{13,9},{2,14},{6,2},{... | collective-permute-start | bytes 12296 | tf_op jit(solution)/shard_map/ppermute | solution.py:209
  46.3 4.6 %collective-permute-start.7 = (f32[8,128]{1,0:T(8,128)S(1)}, f32[8,128]{1,0:T(8,128)S(1)}, u32[]{:S(2)}, u32[]{:S(2)}) collective-permute-start(f32[8,128]{1,0:T(8,128)S(1)} %pad_maximum_fusion.2.refs_5_.refs_0_), channel_id=1, source_target_pairs={{0,8},{4,12},{8,0},{12,4},{1,9},{5,13},{9,1},{13,5},{2,10},{6,14},... | collective-permute-start | bytes 12296 | tf_op jit(solution)/shard_map/ppermute | solution.py:209
  49.9 9.4 %copy-start.11 = (f32[8,128]{1,0:T(8,128)}, f32[8,128]{1,0:T(8,128)S(1)}, u32[]{:S(2)}) copy-start(f32[8,128]{1,0:T(8,128)S(1)} %collective-permute-done.8.refs_8_.refs_3_) | copy-start | bytes 12292
  49.9 9.3 %collective-permute-start.6 = (f32[8,128]{1,0:T(8,128)S(1)}, f32[8,128]{1,0:T(8,128)S(1)}, u32[]{:S(2)}, u32[]{:S(2)}) collective-permute-start(f32[8,128]{1,0:T(8,128)S(1)} %pad_maximum_fusion.2.refs_5_.refs_0_), channel_id=1, source_target_pairs={{0,4},{4,8},{8,12},{12,0},{1,5},{5,9},{9,13},{13,1},{2,6},{6,10},{... | collective-permute-start | bytes 12296 | tf_op jit(solution)/shard_map/ppermute | solution.py:209
  50.9 8.4 %copy-start.12 = (f32[8,128]{1,0:T(8,128)}, f32[8,128]{1,0:T(8,128)S(1)}, u32[]{:S(2)}) copy-start(f32[8,128]{1,0:T(8,128)S(1)} %collective-permute-done.7.refs_7_.refs_2_) | copy-start | bytes 12292
  50.9 29.2 %collective-permute-start.12 = (bf16[3,128,768]{2,1,0:T(8,128)(2,1)S(1)}, bf16[3,128,768]{2,1,0:T(8,128)(2,1)S(1)}, u32[]{:S(2)}, u32[]{:S(2)}) collective-permute-start(bf16[3,128,768]{2,1,0:T(8,128)(2,1)S(1)} %pad_maximum_fusion.1.refs_1_), channel_id=1, source_target_pairs={{0,1},{1,0},{2,3},{3,2},{4,5},{5,4},{6,7},{7,6},{8,9},{9,8},{10,11... | collective-permute-start | bytes 1769480 | tf_op jit(solution)/shard_map/ppermute | solution.py:180
  59.2 20.9 %copy-start.7 = (bf16[3,128,768]{2,1,0:T(8,128)(2,1)}, bf16[3,128,768]{2,1,0:T(8,128)(2,1)S(1)}, u32[]{:S(2)}) copy-start(bf16[3,128,768]{2,1,0:T(8,128)(2,1)S(1)} %collective-permute-done.13.refs_3_) | copy-start | bytes 1769476
  59.2 21.0 %collective-permute-start.14 = (bf16[3,128,768]{2,1,0:T(8,128)(2,1)S(1)}, bf16[3,128,768]{2,1,0:T(8,128)(2,1)S(1)}, u32[]{:S(2)}, u32[]{:S(2)}) collective-permute-start(bf16[3,128,768]{2,1,0:T(8,128)(2,1)S(1)} %collective-permute-done.13.refs_3_), channel_id=1, source_target_pairs={{0,1},{1,0},{2,3},{3,2},{4,5},{5,4},{6,7},{7,6},{8,9},{9,8},{10,11... | collective-permute-start | bytes 1769480 | tf_op jit(solution)/shard_map/ppermute | solution.py:180
  80.2 1.0 copy-start.9
  103.9 8.2 %collective-permute-start.16 = (bf16[4,128,768]{2,1,0:T(8,128)(2,1)}, bf16[4,128,768]{2,1,0:T(8,128)(2,1)S(1)}, u32[]{:S(2)}, u32[]{:S(2)}) collective-permute-start(bf16[4,128,768]{2,1,0:T(8,128)(2,1)} %shard_map.109), channel_id=1, source_target_pairs={{0,1},{1,0},{2,3},{3,2},{4,5},{5,4},{6,7},{7,6},{8,9},{9,8},{10,11... | collective-permute-start | bytes 2359304 | tf_op jit(solution)/shard_map/ppermute | solution.py:274
  112.0 37.1 %collective-permute-start.15 = (bf16[4,128,768]{2,1,0:T(8,128)(2,1)}, bf16[4,128,768]{2,1,0:T(8,128)(2,1)S(1)}, u32[]{:S(2)}, u32[]{:S(2)}) collective-permute-start(bf16[4,128,768]{2,1,0:T(8,128)(2,1)} %shard_map.107), channel_id=1, source_target_pairs={{0,1},{1,0},{2,3},{3,2},{4,5},{5,4},{6,7},{7,6},{8,9},{9,8},{10,11... | collective-permute-start | bytes 2359304 | tf_op jit(solution)/shard_map/ppermute | solution.py:274
  112.1 0.9 copy-start.2
  120.8 37.1 %collective-permute-start.17 = (bf16[4,128,768]{2,1,0:T(8,128)(2,1)}, bf16[4,128,768]{2,1,0:T(8,128)(2,1)S(1)}, u32[]{:S(2)}, u32[]{:S(2)}) collective-permute-start(bf16[4,128,768]{2,1,0:T(8,128)(2,1)} %shard_map.110), channel_id=1, source_target_pairs={{0,2},{2,0},{1,3},{3,1},{4,6},{6,4},{5,7},{7,5},{8,10},{10,8},{9,1... | collective-permute-start | bytes 2359304 | tf_op jit(solution)/shard_map/ppermute | solution.py:279
  149.2 0.9 copy-start.3
  159.3 15.4 %collective-permute-start.18 = (bf16[128,768]{1,0:T(8,128)(2,1)S(1)}, bf16[128,768]{1,0:T(8,128)(2,1)S(1)}, u32[]{:S(2)}, u32[]{:S(2)}) collective-permute-start(bf16[128,768]{1,0:T(8,128)(2,1)S(1)} %get-tuple-element.20), channel_id=1, source_target_pairs={{0,12},{4,0},{8,4},{12,8},{1,13},{5,1},{9,5},{13,9},{2,14},{6,2},{... | collective-permute-start | bytes 589832 | tf_op jit(solution)/shard_map/ppermute | solution.py:286
  159.4 15.3 %collective-permute-start.20 = (bf16[128,768]{1,0:T(8,128)(2,1)S(1)}, bf16[128,768]{1,0:T(8,128)(2,1)S(1)}, u32[]{:S(2)}, u32[]{:S(2)}) collective-permute-start(bf16[128,768]{1,0:T(8,128)(2,1)S(1)} %get-tuple-element.21), channel_id=1, source_target_pairs={{0,4},{4,8},{8,12},{12,0},{1,5},{5,9},{9,13},{13,1},{2,6},{6,10},{... | collective-permute-start | bytes 589832 | tf_op jit(solution)/shard_map/ppermute | solution.py:286
  161.4 17.6 %collective-permute-start.19 = (bf16[128,768]{1,0:T(8,128)(2,1)S(1)}, bf16[128,768]{1,0:T(8,128)(2,1)S(1)}, u32[]{:S(2)}, u32[]{:S(2)}) collective-permute-start(bf16[128,768]{1,0:T(8,128)(2,1)S(1)} %get-tuple-element.22), channel_id=1, source_target_pairs={{0,8},{4,12},{8,0},{12,4},{1,9},{5,13},{9,1},{13,5},{2,10},{6,14},... | collective-permute-start | bytes 589832 | tf_op jit(solution)/shard_map/ppermute | solution.py:286
  (4 other events, 3.2 us)

commit v2 on v0

v2 whole, which is shorter than its diff:
```python
import functools

import jax
import jax.numpy as jnp
from jax import lax
from jax.experimental import pallas as pl
from jax.experimental.pallas import tpu as pltpu
from jax.sharding import PartitionSpec as P

CAP = 72
VM = pltpu.VMEM
F32 = jnp.float32
BF16 = jnp.bfloat16
NN = (((1,), (0,)), ((), ()))
NT = (((1,), (1,)), ((), ()))
TN = (((0,), (0,)), ((), ()))


def mm(a, b, dims):
    return lax.dot_general(a, b, dims, preferred_element_type=F32)


def params(mib):
    return pltpu.CompilerParams(vmem_limit_bytes=mib * 1024 * 1024)


def cost(flops, nbytes):
    return pl.CostEstimate(flops=int(flops), bytes_accessed=int(nbytes), transcendentals=0)


def vmem(count):
    return [pl.BlockSpec(memory_space=VM)] * count


def far(array):
    return pltpu.with_memory_space_constraint(array, pltpu.HBM)


def anywhere(count):
    return [pl.BlockSpec(memory_space=pl.ANY)] * count


def hbm(count):
    return [pl.BlockSpec(memory_space=pltpu.HBM)] * count


SCALARS = pl.BlockSpec(memory_space=pltpu.SMEM)


def shift(count, by):
    return [(i, (i + by) % count) for i in range(count)]


def pair_rows(metas, row, pair):
    first = metas[2 * pair][pl.ds(row, 1), :]
    second = metas[2 * pair + 1][pl.ds(row, 1), :]
    return first, second


def pair_one_hot(metas, expert, pair):
    first, second = pair_rows(metas, expert, pair)
    second = jnp.where(second >= 0, second + CAP, second)
    slot = jnp.concatenate([first, second], axis=1)
    rows = lax.broadcasted_iota(jnp.int32, (2 * CAP, slot.shape[1]), 0).astype(F32)
    return rows == slot


class Gathered:
    def __init__(self, refs, pieces):
        self.own = refs[0]
        self.pieces = list(zip(pieces, refs[1:]))

    def pack(self, here, exp_count, slab, pair, hot, scale, store):
        for (dx, dc, offset), ref in self.pieces:
            x = lax.rem(here[0] + exp_count - dx, exp_count)
            c = lax.rem(here[1] + dc, 2)
            width = ref.shape[2]
            column = pl.multiple_of((x * 2 + c) * slab + offset, 128)
            if pair == 0:
                rows = jnp.concatenate([self.own[:, pl.ds(column, width)], ref[0]], axis=0)
            else:
                rows = jnp.concatenate([ref[2 * pair - 1], ref[2 * pair]], axis=0)
            packed = mm(hot, rows, NN)
            if scale is not None:
                packed = packed * scale
            store(column, width, packed.astype(BF16))


def start_all(copies):
    for copy in copies:
        copy.start()


def wait_all(copies):
    for copy in copies:
        copy.wait()


class Saves:
    def __init__(self, sems):
        self.sems, self.copies = sems, []

    def __call__(self, src, dst):
        copy = pltpu.make_async_copy(src, dst, self.sems.at[len(self.copies)])
        copy.start()
        self.copies.append(copy)


def load_all(srcs, dsts, sems):
    return [pltpu.make_async_copy(src, dst, sems.at[k]) for k, (src, dst) in enumerate(zip(srcs, dsts))]


def forward_kernel(n, exp_count, pieces, slab, tile, local, here_ref, *refs):
    metas, refs = refs[:n], refs[n:]
    loads, refs = refs[:1 + len(pieces)], refs[1 + len(pieces):]
    gate_hbm, up_hbm, xp_out, hid_out, act_out, dact_out = refs[:6]
    staged, refs = refs[6:6 + len(loads)], refs[6 + len(loads):]
    xp_ref, hid_ref, act_ref, dact_ref, gate_w, up_w, load_sems, sems, save_sems = refs
    data = Gathered(staged, pieces)
    steps = gate_hbm.shape[2] // tile
    ring = gate_w.shape[0]
    expert = here_ref[0] * gate_hbm.shape[0] + local

    def fetch(j):
        units = pl.ds(j * tile, tile)
        return [
            pltpu.make_async_copy(src.at[local, :, units], dst.at[j % ring], sems.at[k, j % ring])
            for k, (src, dst) in enumerate(((gate_hbm, gate_w), (up_hbm, up_w)))
        ]

    first = load_all(loads, staged, load_sems)
    save = Saves(save_sems)
    start_all(first)
    start_all(fetch(0))
    wait_all(first)
    for j in range(1, min(ring, steps)):
        start_all(fetch(j))
    for pair in range(n // 2):
        hot = pair_one_hot(metas, expert, pair).astype(BF16)

        def store(column, width, value):
            xp_ref[pl.ds(pair * 2 * CAP, 2 * CAP), pl.ds(column, width)] = value

        data.pack(here_ref, exp_count, slab, pair, hot, None, store)
    save(xp_ref, xp_out)
    for j in range(steps):
        wait_all(fetch(j))
        units = pl.ds(j * tile, tile)
        rows = xp_ref[...]
        gate = mm(rows, gate_w[j % ring], NN)
        up = mm(rows, up_w[j % ring], NN)
        if j + ring < steps:
            start_all(fetch(j + ring))
        sig = jax.nn.sigmoid(gate)
        act = gate * sig
        hid_ref[:, units] = (act * up).astype(BF16)
        act_ref[:, units] = act
        dact_ref[:, units] = up * sig * (1.0 + gate * (1.0 - sig))
        save(act_ref.at[:, units], act_out.at[:, units])
        save(dact_ref.at[:, units], dact_out.at[:, units])
    save(hid_ref, hid_out)
    wait_all(save.copies)


def slab_chunks(here_ref, gate_hbm, up_hbm, gate_w, up_w, sems, slabs):
    ring, width, _ = gate_w.shape
    chunks = []
    for s in range(slabs):
        rows = pl.ds(pl.multiple_of(here_ref[2 + s] * width, 128), width)
        for e in range(gate_hbm.shape[0]):
            k = len(chunks) % ring
            chunks.append([
                pltpu.make_async_copy(src.at[e, rows, :], dst.at[k], sems.at[m, k])
                for m, (src, dst) in enumerate(((gate_hbm, gate_w), (up_hbm, up_w)))
            ])
    return chunks


def slab_rows(n, here_ref, metas, gg_ref, ug_ref, gate_w, up_w, stream, used, out_ref, save):
    local_count = gg_ref.shape[0]
    ring = gate_w.shape[0]
    begun = used
    for s in range(out_ref.shape[0]):
        terms = []
        for local in range(local_count):
            wait_all(stream[used])
            k = (used - begun) % ring
            term = mm(gg_ref[local], gate_w[k], NT) + mm(ug_ref[local], up_w[k], NT)
            terms.append(term.astype(BF16))
            if used + ring < len(stream):
                start_all(stream[used + ring])
            used += 1
        for pair in range(n // 2):
            total = None
            for local, term in enumerate(terms):
                expert = here_ref[0] * local_count + local
                hot = pair_one_hot(metas, expert, pair).astype(BF16)
                part = mm(hot, term[pair * 2 * CAP:(pair + 1) * 2 * CAP], TN)
                total = part if total is None else total + part
            half = total.shape[0] // 2
            for j in range(2):
                out_ref[s, (2 * pair + j - 1) % n] = total[j * half:(j + 1) * half].astype(BF16)
        save(out_ref.at[s], s)


def backward_kernel(n, exp_count, pieces, slab, tile, local_count, slabs, here_ref, *refs):
    metas, refs = refs[:n], refs[n:]
    loads, refs = refs[:1 + len(pieces)], refs[1 + len(pieces):]
    act_hbm, refs = refs[:2 * local_count], refs[2 * local_count:]
    gate_hbm, up_hbm, down_hbm, gp_hbm, gg_hbm, ug_hbm, gg_ref, ug_ref = refs[:8]
    outs, refs = refs[8:8 + slabs], refs[8 + slabs:]
    staged, refs = refs[:len(loads)], refs[len(loads):]
    (act_ref, dact_ref, gp_ref, out_ref, gate_w, up_w, down_w,
     load_sems, act_sems, slab_sems, down_sems, save_sems) = refs
    data = Gathered(staged, pieces)
    steps = gg_ref.shape[2] // tile
    ring = gate_w.shape[0]

    first = load_all(loads, staged, load_sems)
    scales = []
    for e in range(local_count):
        scales.append([
            pltpu.make_async_copy(act_hbm[e], act_ref.at[e], act_sems.at[0, e]),
            pltpu.make_async_copy(act_hbm[local_count + e], dact_ref.at[e], act_sems.at[1, e]),
        ])
    downs = []
    for e in range(local_count):
        for j in range(steps):
            k = len(downs) % ring
            src = down_hbm.at[e, pl.ds(j * tile, tile), :]
            downs.append([pltpu.make_async_copy(src, down_w.at[k], down_sems.at[k])])
    stream = downs + slab_chunks(here_ref, gate_hbm, up_hbm, gate_w, up_w, slab_sems, slabs)
    save = Saves(save_sems)

    start_all(first)
    start_all(stream[0])
    wait_all(first)
    start_all(scales[0])
    for copies in stream[1:ring]:
        start_all(copies)
    for copies in scales[1:]:
        start_all(copies)
    experts = local_count * exp_count
    used = 0
    for local in range(local_count):
        expert = here_ref[0] * local_count + local
        for pair in range(n // 2):
            hot = pair_one_hot(metas, expert, pair)
            weights = jnp.concatenate(pair_rows(metas, experts + expert, pair), axis=1)
            scale = jnp.sum(jnp.where(hot, weights, 0.0), axis=1, keepdims=True)

            def store(column, width, value):
                gp_ref[local, pl.ds(pair * 2 * CAP, 2 * CAP), pl.ds(column, width)] = value

            data.pack(here_ref, exp_count, slab, pair, hot.astype(BF16), scale, store)
        save(gp_ref.at[local], gp_hbm.at[local])
        wait_all(scales[local])
        for j in range(steps):
            wait_all(stream[used])
            units = pl.ds(j * tile, tile)
            hidden_grad = mm(gp_ref[local], down_w[used % ring], NT)
            ug_ref[local, :, units] = (hidden_grad * act_ref[local, :, units]).astype(BF16)
            gg_ref[local, :, units] = (hidden_grad * dact_ref[local, :, units]).astype(BF16)
            if used + ring < len(stream):
                start_all(stream[used + ring])
            used += 1
        save(gg_ref.at[local], gg_hbm.at[local])
        save(ug_ref.at[local], ug_hbm.at[local])
    slab_rows(n, here_ref, metas, gg_ref, ug_ref, gate_w, up_w, stream, used, out_ref,
              lambda src, s: save(src, outs[s]))
    wait_all(save.copies)


def home_kernel(n, slabs, here_ref, *refs):
    metas, refs = refs[:n], refs[n:]
    gg_ref, ug_ref, gate_hbm, up_hbm = refs[:4]
    outs = refs[4:4 + slabs]
    out_ref, gate_w, up_w, slab_sems, save_sems = refs[4 + slabs:]
    stream = slab_chunks(here_ref, gate_hbm, up_hbm, gate_w, up_w, slab_sems, slabs)
    save = Saves(save_sems)
    for copies in stream[:gate_w.shape[0]]:
        start_all(copies)
    slab_rows(n, here_ref, metas, gg_ref, ug_ref, gate_w, up_w, stream, 0, out_ref,
              lambda src, s: save(src, outs[s]))
    wait_all(save.copies)


def hold_kernel(*refs):
    del refs


def hold(arrays, after):
    return pl.pallas_call(
        hold_kernel,
        out_shape=[jax.ShapeDtypeStruct(a.shape, a.dtype) for a in arrays],
        in_specs=anywhere(len(arrays) + len(after)),
        out_specs=anywhere(len(arrays)),
        input_output_aliases={k: k for k in range(len(arrays))},
        compiler_params=params(4),
        cost_estimate=cost(0, 0),
    )(*arrays, *after)


def weights_kernel(counts, xp_ref, hid_ref, gg_ref, ug_ref, gp_ref, *refs):
    gate_out, up_out, down_out = refs[-3:]
    step = pl.program_id(0)
    tile = gate_out.shape[1]

    def columns(at):
        return pl.ds(pl.multiple_of(at * tile, 128), tile)

    @pl.when(step < counts)
    def _():
        gate_out[0] = mm(xp_ref[:, columns(step)], gg_ref[0], TN).astype(BF16)

    @pl.when(jnp.logical_and(step >= counts, step < 2 * counts))
    def _():
        up_out[0] = mm(xp_ref[:, columns(step - counts)], ug_ref[0], TN).astype(BF16)

    @pl.when(step >= 2 * counts)
    def _():
        down_out[0] = mm(hid_ref[...], gp_ref[0, :, columns(step - 2 * counts)], TN).astype(BF16)


def weight_grads(local, xp, hidden, gate_grad, up_grad, gp, before):
    slots, depth = xp.shape
    local_count, _, hidden_units = gate_grad.shape
    tile = 1024
    counts = depth // tile
    shapes = [(local_count, depth, hidden_units)] * 2 + [(local_count, hidden_units, depth)]

    def place(which, step):
        return jnp.clip(step - which * counts, 0, counts - 1)

    one = lambda array: pl.BlockSpec((1, *array.shape[1:]), lambda i: (local, 0, 0))
    all_of = lambda array: pl.BlockSpec(array.shape, lambda i: (0, 0))
    return pl.pallas_call(
        functools.partial(weights_kernel, counts),
        out_shape=[jax.ShapeDtypeStruct(shape, BF16) for shape in shapes],
        grid=(3 * counts,),
        in_specs=[all_of(xp), all_of(hidden), one(gate_grad), one(up_grad), one(gp)]
        + anywhere(len(before)),
        out_specs=[
            pl.BlockSpec((1, tile, hidden_units), lambda i: (local, place(0, i), 0)),
            pl.BlockSpec((1, tile, hidden_units), lambda i: (local, place(1, i), 0)),
            pl.BlockSpec((1, hidden_units, tile), lambda i: (local, 0, place(2, i))),
        ],
        input_output_aliases={5 + k: k for k in range(len(before))},
        compiler_params=params(40),
        cost_estimate=cost(6 * slots * depth * hidden_units, 6 * depth * hidden_units),
    )(far(xp), far(hidden), far(gate_grad), far(up_grad), far(gp), *before)


def gather_ctx(mine, n):
    return [lax.ppermute(mine, "ctx", shift(n, s)) for s in range(1, n)]


def exchange(received, exp_count):
    others = jnp.stack(received)
    return others, [lax.ppermute(others, "exp", shift(exp_count, dx)) for dx in range(1, exp_count)]


def siblings(parts, offset):
    pieces, arrays = [], []
    for dx, part in enumerate(parts):
        pieces += [(dx, 0, offset), (dx, 1, offset)]
        arrays += [part, lax.ppermute(part, "tp", shift(2, 1))]
    return pieces, arrays


def per_device(tokens, out_grad, expert_ids, gate_weights, gate_matrix, up_matrix, down_matrix):
    n = lax.axis_size("ctx")
    exp_count = lax.axis_size("exp")
    x = lax.axis_index("exp")
    c = lax.axis_index("tp")
    local_count, depth, hidden_units = gate_matrix.shape
    experts = local_count * exp_count
    block, _ = tokens.shape
    width = depth // (exp_count * 2)
    slots = n * CAP
    here = jnp.stack([x, c, (x * 2 + c) * width, 0]).astype(jnp.int32)

    names = jnp.arange(experts, dtype=jnp.int32)[:, None]
    chosen = [expert_ids[:, k][None, :] == names for k in range(expert_ids.shape[1])]
    member = functools.reduce(jnp.logical_or, chosen)
    before = jnp.arange(block)[:, None] <= jnp.arange(block)[None, :]
    order = jnp.dot(member.astype(BF16), before.astype(BF16), preferred_element_type=F32)
    slot = jnp.where(member, order - 1.0, -1.0)
    weight = sum(jnp.where(ch, gate_weights[:, k][None, :], 0.0) for k, ch in enumerate(chosen))
    meta = jnp.concatenate([slot, weight], axis=0)

    half = width // 256 * 128
    cuts = [(0, half), (half, width - half)]

    def mine(array, piece):
        offset, size = cuts[piece]
        return lax.dynamic_slice_in_dim(array, (x * 2 + c) * width + offset, size, axis=1)

    m = n - 1
    step = hold(gather_ctx(mine(tokens, 0), n) + gather_ctx(meta, n), [])
    t0, metas = step[:m], [meta, *step[m:]]
    t0, t0_exp = exchange(t0, exp_count)
    step = hold(gather_ctx(mine(tokens, 1), n) + t0_exp, [])
    t1, t0_exp = step[:m], step[m:]
    t1, t1_exp = exchange(t1, exp_count)
    t_pieces, t_arrays = siblings([t0, *t0_exp], 0)
    step = hold(gather_ctx(mine(out_grad, 0), n) + t1_exp, t_arrays)
    g0, t1_exp = step[:m], step[m:]
    g0, g0_exp = exchange(g0, exp_count)
    more_pieces, more_arrays = siblings([t1, *t1_exp], half)
    t_pieces += more_pieces
    t_arrays += more_arrays
    g1 = gather_ctx(mine(out_grad, 1), n)

    tile = min(512, hidden_units)
    fine = min(256, hidden_units)
    flops = 2 * local_count * slots * depth * hidden_units
    dma = pltpu.SemaphoreType.DMA
    stack = lambda cols, dtype: pltpu.HBM((slots, cols), dtype)
    near = lambda shape: pltpu.HBM(shape, BF16)
    loads = [tokens, *t_arrays]
    forward = []
    for local in range(local_count):
        forward.append(pl.pallas_call(
            functools.partial(forward_kernel, n, exp_count, t_pieces, width, fine, local),
            out_shape=(stack(depth, BF16), stack(hidden_units, BF16),
                       stack(hidden_units, F32), stack(hidden_units, F32)),
            in_specs=[SCALARS] + vmem(n) + anywhere(len(loads)) + hbm(2),
            out_specs=hbm(4),
            scratch_shapes=[VM(a.shape, BF16) for a in loads]
            + [VM((slots, depth), BF16), VM((slots, hidden_units), BF16)]
            + [VM((slots, hidden_units), F32)] * 2 + [VM((2, depth, fine), BF16)] * 2
            + [dma((len(loads),)), dma((2, 2)), dma((2 + 2 * (hidden_units // fine),))],
            compiler_params=params(34),
            cost_estimate=cost(2 * flops // local_count, 0),
        )(here, *metas, *loads, far(gate_matrix), far(up_matrix)))
        if local == 0:
            step = hold(g1 + g0_exp, forward[0][2:3])
            g1, g0_exp = step[:m], step[m:]
            g1, g1_exp = exchange(g1, exp_count)
    xps, hiddens, acts, dacts = zip(*forward)
    g1_exp = hold(g1_exp, acts[1:])
    g_pieces, g_arrays = siblings([g0, *g0_exp], 0)
    more_pieces, more_arrays = siblings([g1, *g1_exp], half)
    g_pieces += more_pieces
    g_arrays += more_arrays

    away = [(dx, dc) for dx in range(1, exp_count) for dc in (1, 0)]
    home = [(0, 1), (0, 0)]

    def where(slabs):
        at = [lax.rem(x + dx, exp_count) * 2 + lax.rem(c + dc, 2) for dx, dc in slabs]
        return jnp.stack([x, c, *at]).astype(jnp.int32)

    part = (n, block, width)
    units = (local_count, slots, hidden_units)
    ring = 3
    slab_buffers = [VM((ring, width, hidden_units), BF16)] * 2
    loads = [out_grad, *g_arrays]
    gp, gate_grad, up_grad, gate_near, up_near, *away_outs = pl.pallas_call(
        functools.partial(
            backward_kernel, n, exp_count, g_pieces, width, tile, local_count, len(away)
        ),
        out_shape=[near((local_count, slots, depth)), near(units), near(units)]
        + [VM(units, BF16)] * 2 + [near(part)] * len(away),
        in_specs=[SCALARS] + vmem(n) + anywhere(len(loads)) + hbm(2 * local_count + 3),
        out_specs=hbm(3) + vmem(2) + hbm(len(away)),
        scratch_shapes=[VM(a.shape, BF16) for a in loads]
        + [VM(units, F32)] * 2 + [VM((local_count, slots, depth), BF16)]
        + [VM((len(away), *part), BF16)] + slab_buffers
        + [VM((ring, tile, depth), BF16), dma((len(loads),)), dma((2, local_count)),
           dma((2, ring)), dma((ring,)), dma((3 * local_count + len(away),))],
        compiler_params=params(48),
        cost_estimate=cost(2 * flops, 0),
    )(
        where(away), *metas, *loads, *map(far, acts), *map(far, dacts),
        far(gate_matrix), far(up_matrix), far(down_matrix),
    )
    away_outs = dict(zip(away, away_outs))
    early = n // 2

    def chip_sum(outs, dx, rows, sibling):
        return outs[dx, 0][rows].astype(F32) + sibling[rows].astype(F32)

    parts = [slice(0, early), slice(early, n)]
    arrived = [[], []]
    for dx in range(1, exp_count):
        sibling = lax.ppermute(away_outs[dx, 1], "tp", shift(2, 1))
        for k, rows in enumerate(parts):
            out = chip_sum(away_outs, dx, rows, sibling).astype(BF16)
            arrived[k].append(lax.ppermute(out, "exp", shift(exp_count, dx)))

    home_outs = pl.pallas_call(
        functools.partial(home_kernel, n, len(home)),
        out_shape=[near(part)] * len(home),
        in_specs=[SCALARS] + vmem(n + 2) + hbm(2),
        out_specs=hbm(len(home)),
        scratch_shapes=[VM((len(home), *part), BF16)] + slab_buffers
        + [dma((2, ring)), dma((len(home),))],
        compiler_params=params(22),
        cost_estimate=cost(4 * flops * width // depth, 0),
    )(where(home), *metas, gate_near, up_near, far(gate_matrix), far(up_matrix))
    home_outs = dict(zip(home, home_outs))
    sibling = lax.ppermute(home_outs[0, 1], "tp", shift(2, 1))
    final = None
    for k, rows in enumerate(parts):
        total = chip_sum(home_outs, 0, rows, sibling)
        for other in arrived[k]:
            total = total + other.astype(F32)
        rounded = total.astype(BF16)
        for j in range(total.shape[0]):
            s = rows.start + j + 1
            if s < n:
                term = lax.ppermute(rounded[j], "ctx", shift(n, -s)).astype(F32)
            else:
                term = total[j]
            final = term if final is None else final + term
    grad_tokens = final.astype(BF16)

    grads = []
    for local in range(local_count):
        grads = weight_grads(
            local, xps[local], hiddens[local], gate_grad, up_grad, gp, grads
        )
    grad_gate, grad_up, grad_down = grads
    return (grad_gate, grad_up, grad_down, grad_tokens)


def solution(mesh):
    in_specs = (
        P(("groups", "ctx"), None),
        P(("groups", "ctx"), None),
        P(("groups", "ctx"), None),
        P(("groups", "ctx"), None),
        P("exp", None, ("ctx", "tp")),
        P("exp", None, ("ctx", "tp")),
        P("exp", ("ctx", "tp"), None),
    )
    out_specs = (
        P(("groups", "exp"), None, ("ctx", "tp")),
        P(("groups", "exp"), None, ("ctx", "tp")),
        P(("groups", "exp"), ("ctx", "tp"), None),
        P(("groups", "ctx"), ("exp", "tp")),
    )
    return jax.shard_map(
        per_device, mesh=mesh, in_specs=in_specs, out_specs=out_specs, check_vma=False
    )
```

time: 305 us -> 155 us (0.51); the launches traced: 299 us -> 154 us
  waiting for transfers between devices: 145 us -> 21.7 us
  Pallas kernels: 0 us -> 84.8 us
  matrix products: 81.1 us -> 0.13 us
  other arithmetic: 25.3 us -> 1.64 us
  starting transfers between devices: 10.1 us -> 31.4 us
  between operations: 14.6 us -> 0.94 us
  local copies, waits for them, and re-layouts: 22.8 us -> 13.7 us
    all_gather x2 -> x0, waiting for transfers between devices: 131 us -> none  [the longest x1 71.7 us: per_device(): lax.all_gather(local_tokens, 'ctx', axis=1, tiled=True)]
    pallas_call x0 -> x11, Pallas kernels: none -> 84.8 us  [the longest x2 35 us: weight_grads(): pl.pallas_call(functools.partial(weights_kernel, counts), out_shape=[jax....]
    dot_general x16 -> x1, matrix products: 81.1 us -> 0.13 us  [per_device(): jnp.dot(member.astype(BF16), before.astype(BF16), preferred_element_type=...]
    ppermute x0 -> x34, starting transfers between devices: none -> 31.4 us  [the longest x15 19.7 us: gather_ctx(): return [lax.ppermute(mine, 'ctx', shift(n, s)) for s in range(1, n)]]
    ppermute x0 -> x34, waiting for transfers between devices: none -> 21.7 us  [the longest x15 21.5 us: gather_ctx(): return [lax.ppermute(mine, 'ctx', shift(n, s)) for s in range(1, n)]]
    another operation x10 -> x7, other arithmetic: 20.4 us -> 0.4 us  [the longest x4 0.18 us: exchange(): others = jnp.stack(received)]
    reduce_scatter x2 -> x0, waiting for transfers between devices: 13.8 us -> none  [the longest x1 10.1 us: per_device(): lax.psum_scatter(complete.astype(jnp.bfloat16), 'tp', scatter_dimension=3...]
    reduce_scatter x2 -> x0, starting transfers between devices: 9.96 us -> none  [the longest x1 9.92 us: per_device(): lax.psum_scatter(summed.astype(jnp.bfloat16), 'exp', scatter_dimension=1,...]
  transfers between devices with their start and end apart: 5 -> 34, of which waited for: 4 -> 9; matrix products, arithmetic and copies ran while one was open for 19% -> 2% of each run, Pallas kernels for 0% -> 43%
where the time goes in v2:
time: 155 us; the launch traced here: 154 us
  Pallas kernels  84.8 us (55%)
  starting transfers between devices  31.4 us (20%)
  waiting for transfers between devices  21.7 us (14%)
  local copies, waits for them, and re-layouts  13.7 us (9%)
  other arithmetic  1.64 us (1%)
    pallas_call x2, Pallas kernels, weight_grads(): pl.pallas_call(functools.partial(weights_kernel, counts), out_shape=[jax....  35 us
    ppermute x15, waiting for transfers between devices, gather_ctx(): return [lax.ppermute(mine, 'ctx', shift(n, s)) for s in range(1, n)]  21.5 us
    pallas_call x2, Pallas kernels, per_device(): pl.pallas_call(functools.partial(forward_kernel, n, exp_count, t_pieces,...  20.5 us
    ppermute x15, starting transfers between devices, gather_ctx(): return [lax.ppermute(mine, 'ctx', shift(n, s)) for s in range(1, n)]  19.7 us
    pallas_call x1, Pallas kernels, per_device(): pl.pallas_call(functools.partial(backward_kernel, n, exp_count, g_pieces,...  19.1 us
    pallas_call x1, Pallas kernels, per_device(): pl.pallas_call(functools.partial(home_kernel, n, len(home)), out_shape=[n...  10.3 us
    unnamed x32, local copies, waits for them, and re-layouts  10.1 us
    ppermute x4, starting transfers between devices, exchange(): lax.ppermute(others, 'exp', shift(exp_count, dx))  4.31 us
  transfers between devices with their start and end apart: 34, of which 9 were waited for; matrix products, arithmetic and copies ran while one was open for 2% of the time, Pallas kernels for 43%

profile of v2, /device:TPU:0, one launch (start us, length us, event | category | flops | bytes accessed | tf_op | source)
XLA Modules:
  0.0 154.2 jit_solution(17097240546118826163)
XLA Ops:
  0.6 1.0 constant_dynamic-slice_fusion.2
  1.7 5.1 %collective-permute-start.2 = (bf16[128,384]{1,0:T(8,128)(2,1)S(1)}, bf16[128,384]{1,0:T(8,128)(2,1)S(1)}, u32[]{:S(2)}, u32[]{:S(2)}) collective-permute-start(bf16[128,384]{1,0:T(8,128)(2,1)S(1)} %get-tuple-element.93), channel_id=1, source_target_pairs={{0,12},{4,0},{8,4},{12,8},{1,13},{5,1},{9,5},{13,9},{2,14},{6,2},{... | collective-permute-start | bytes 294920 | tf_op jit(solution)/shard_map/ppermute | solution.py:355
  6.8 1.0 collective-permute-start
  9.5 2.9 %collective-permute-start.5 = (f32[8,128]{1,0:T(8,128)S(1)}, f32[8,128]{1,0:T(8,128)S(1)}, u32[]{:S(2)}, u32[]{:S(2)}) collective-permute-start(f32[8,128]{1,0:T(8,128)S(1)} %pad_maximum_fusion.4.refs_0_), channel_id=1, source_target_pairs={{0,12},{4,0},{8,4},{12,8},{1,13},{5,1},{9,5},{13,9},{2,14},{6,2},{... | collective-permute-start | bytes 12296 | tf_op jit(solution)/shard_map/ppermute | solution.py:355
  12.3 1.1 collective-permute-start.4
  14.0 2.3 %collective-permute-start.3 = (f32[8,128]{1,0:T(8,128)S(1)}, f32[8,128]{1,0:T(8,128)S(1)}, u32[]{:S(2)}, u32[]{:S(2)}) collective-permute-start(f32[8,128]{1,0:T(8,128)S(1)} %pad_maximum_fusion.4.refs_0_), channel_id=1, source_target_pairs={{0,4},{4,8},{8,12},{12,0},{1,5},{5,9},{9,13},{13,1},{2,6},{6,10},{... | collective-permute-start | bytes 12296 | tf_op jit(solution)/shard_map/ppermute | solution.py:355
  16.8 2.6 %collective-permute-done.3.refs_3_ = f32[8,128]{1,0:T(8,128)S(1)} collective-permute-done((f32[8,128]{1,0:T(8,128)S(1)}, f32[8,128]{1,0:T(8,128)S(1)}, u32[]{:S(2)}, u32[]{:S(2)}) %collective-permute-start.3) | collective-permute-done | bytes 4128 | tf_op jit(solution)/shard_map/ppermute | solution.py:355
  19.5 1.6 %collective-permute-start.10 = (bf16[3,128,384]{2,1,0:T(8,128)(2,1)S(1)}, bf16[3,128,384]{2,1,0:T(8,128)(2,1)S(1)}, u32[]{:S(2)}, u32[]{:S(2)}) collective-permute-start(bf16[3,128,384]{2,1,0:T(8,128)(2,1)S(1)} %pad_maximum_fusion.refs_4_.refs_5_), channel_id=1, source_target_pairs={{0,2},{2,0},{1,3},{3,1},{4,6},{6,4},{5,7},{7,5},{8,10},{10,8},{9,1... | collective-permute-start | bytes 884744 | tf_op jit(solution)/shard_map/ppermute | solution.py:360
  21.1 2.0 %collective-permute-start.9 = (bf16[128,384]{1,0:T(8,128)(2,1)S(1)}, bf16[128,384]{1,0:T(8,128)(2,1)S(1)}, u32[]{:S(2)}, u32[]{:S(2)}) collective-permute-start(bf16[128,384]{1,0:T(8,128)(2,1)S(1)} %get-tuple-element.92), channel_id=1, source_target_pairs={{0,12},{4,0},{8,4},{12,8},{1,13},{5,1},{9,5},{13,9},{2,14},{6,2},{... | collective-permute-start | bytes 294920 | tf_op jit(solution)/shard_map/ppermute | solution.py:355
  23.7 3.5 %collective-permute-done.9.refs_2_ = bf16[128,384]{1,0:T(8,128)(2,1)S(1)} collective-permute-done((bf16[128,384]{1,0:T(8,128)(2,1)S(1)}, bf16[128,384]{1,0:T(8,128)(2,1)S(1)}, u32[]{:S(2)}, u32[]{:S(2)}) %collective-permute-start.9) | collective-permute-done | bytes 98336 | tf_op jit(solution)/shard_map/ppermute | solution.py:355
  27.2 3.1 %collective-permute-done.8.refs_1_ = bf16[128,384]{1,0:T(8,128)(2,1)S(1)} collective-permute-done((bf16[128,384]{1,0:T(8,128)(2,1)S(1)}, bf16[128,384]{1,0:T(8,128)(2,1)S(1)}, u32[]{:S(2)}, u32[]{:S(2)}) %collective-permute-start.8) | collective-permute-done | bytes 98336 | tf_op jit(solution)/shard_map/ppermute | solution.py:355
  31.0 1.0 constant_dynamic-slice_fusion
  31.9 1.3 collective-permute-start.15
  33.4 4.7 %collective-permute-done.15.refs_2_ = bf16[128,384]{1,0:T(8,128)(2,1)S(1)} collective-permute-done((bf16[128,384]{1,0:T(8,128)(2,1)S(1)}, bf16[128,384]{1,0:T(8,128)(2,1)S(1)}, u32[]{:S(2)}, u32[]{:S(2)}) %collective-permute-start.15) | collective-permute-done | bytes 98336 | tf_op jit(solution)/shard_map/ppermute | solution.py:355
  38.1 3.0 %collective-permute-done.14.refs_1_ = bf16[128,384]{1,0:T(8,128)(2,1)S(1)} collective-permute-done((bf16[128,384]{1,0:T(8,128)(2,1)S(1)}, bf16[128,384]{1,0:T(8,128)(2,1)S(1)}, u32[]{:S(2)}, u32[]{:S(2)}) %collective-permute-start.14) | collective-permute-done | bytes 98336 | tf_op jit(solution)/shard_map/ppermute | solution.py:355
  41.1 3.4 %collective-permute-done.13.refs_0_ = bf16[128,384]{1,0:T(8,128)(2,1)S(1)} collective-permute-done((bf16[128,384]{1,0:T(8,128)(2,1)S(1)}, bf16[128,384]{1,0:T(8,128)(2,1)S(1)}, u32[]{:S(2)}, u32[]{:S(2)}) %collective-permute-start.13) | collective-permute-done | bytes 98336 | tf_op jit(solution)/shard_map/ppermute | solution.py:355
  44.7 1.9 %collective-permute-start.21 = (bf16[128,384]{1,0:T(8,128)(2,1)S(1)}, bf16[128,384]{1,0:T(8,128)(2,1)S(1)}, u32[]{:S(2)}, u32[]{:S(2)}) collective-permute-start(bf16[128,384]{1,0:T(8,128)(2,1)S(1)} %get-tuple-element.90), channel_id=1, source_target_pairs={{0,12},{4,0},{8,4},{12,8},{1,13},{5,1},{9,5},{13,9},{2,14},{6,2},{... | collective-permute-start | bytes 294920 | tf_op jit(solution)/shard_map/ppermute | solution.py:355
  46.6 1.3 collective-permute-start.19
  48.0 1.6 %collective-permute-start.22 = (bf16[3,128,384]{2,1,0:T(8,128)(2,1)S(1)}, bf16[3,128,384]{2,1,0:T(8,128)(2,1)S(1)}, u32[]{:S(2)}, u32[]{:S(2)}) collective-permute-start(bf16[3,128,384]{2,1,0:T(8,128)(2,1)S(1)} %pad_maximum_fusion.2.refs_5_), channel_id=1, source_target_pairs={{0,2},{2,0},{1,3},{3,1},{4,6},{6,4},{5,7},{7,5},{8,10},{10,8},{9,1... | collective-permute-start | bytes 884744 | tf_op jit(solution)/shard_map/ppermute | solution.py:360
  49.6 10.2 %shard_map.106 = (bf16[288,3072]{1,0:T(8,128)(2,1)}, bf16[288,1024]{1,0:T(8,128)(2,1)}, f32[288,1024]{1,0:T(8,128)}, f32[288,1024]{1,0:T(8,128)}) custom-call(s32[4]{0:T(128)S(1)} %pad_add_fusion.here_ref, f32[8,128]{1,0:T(8,128)S(1)} %pad_maximum_fusion.4.refs_0_, f32[8,128]{1,0:T(8,128)S(1)} %get-tuple-element.45.refs_1_, ...), custom_call_target="tpu_custom_call" | custom-call | flops 3623878656 | tf_op jit(solution)/shard_map/pallas_call | solution.py:424
  59.9 1.3 copy-done
  62.3 10.2 %shard_map.105 = (bf16[288,3072]{1,0:T(8,128)(2,1)}, bf16[288,1024]{1,0:T(8,128)(2,1)}, f32[288,1024]{1,0:T(8,128)}, f32[288,1024]{1,0:T(8,128)}) custom-call(s32[4]{0:T(128)S(1)} %pad_add_fusion.here_ref, f32[8,128]{1,0:T(8,128)S(1)} %pad_maximum_fusion.4.refs_0_, f32[8,128]{1,0:T(8,128)S(1)} %get-tuple-element.45.refs_1_, ...), custom_call_target="tpu_custom_call" | custom-call | flops 3623878656 | tf_op jit(solution)/shard_map/pallas_call | solution.py:424
  72.6 1.3 copy-done.1
  79.4 19.1 %shard_map.109 = (bf16[2,288,3072]{2,1,0:T(8,128)(2,1)}, bf16[2,288,1024]{2,1,0:T(8,128)(2,1)}, bf16[2,288,1024]{2,1,0:T(8,128)(2,1)}, bf16[2,288,1024]{2,1,0:T(...) custom-call(s32[4]{0:T(128)S(1)} %pad_add_fusion.2.here_ref, ...), custom_call_target="tpu_custom_call" | custom-call | flops 7247757312 | tf_op jit(solution)/shard_map/pallas_call | solution.py:460
  98.5 1.0 copy-done.4
  99.9 1.3 copy-done.5
  101.1 10.3 %shard_map.112 = (bf16[4,128,768]{2,1,0:T(8,128)(2,1)}, bf16[4,128,768]{2,1,0:T(8,128)(2,1)}) custom-call(s32[4]{0:T(128)S(1)} %pad_add_fusion.3.here_ref, f32[8,128]{1,0:T(8,128)S(1)} %pad_maximum_fusion.4.refs_0_, f32[8,128]{1,0:T(8,128)S(1)} %get-tuple-element.45.refs_1_, f32[8,128]{1,0:T(8,128)S(1)} %get-tuple-element.46.refs_2_, ...), custom_call_target="tpu_custom_call" | custom-call | flops 3623878656 | tf_op jit(solution)/shard_map/pallas_call | solution.py:493
  112.0 1.6 %collective-permute-start.29 = (bf16[2,128,768]{2,1,0:T(8,128)(2,1)S(1)}, bf16[2,128,768]{2,1,0:T(8,128)(2,1)S(1)}, u32[]{:S(2)}, u32[]{:S(2)}) collective-permute-start(bf16[2,128,768]{2,1,0:T(8,128)(2,1)S(1)} %get-tuple-element.88), channel_id=1, source_target_pairs={{0,2},{2,0},{1,3},{3,1},{4,6},{6,4},{5,7},{7,5},{8,10},{10,8},{9,1... | collective-permute-start | bytes 1179656 | tf_op jit(solution)/shard_map/ppermute | solution.py:491
  114.0 17.5 %shard_map.110 = (bf16[2,3072,1024]{2,1,0:T(8,128)(2,1)}, bf16[2,3072,1024]{2,1,0:T(8,128)(2,1)}, bf16[2,1024,3072]{2,1,0:T(8,128)(2,1)}) custom-call(bf16[288,3072]{1,0:T(8,128)(2,1)} %get-tuple-element.72.xp_ref, bf16[288,1024]{1,0:T(8,128)(2,1)} %get-tuple-element.73.hid_ref, bf16[2,288,1024]{2,1,0:T(8,128)(2,1)} %get-tuple-element.69.gg_ref, ...), custom_call_target="tpu_custom_call" | custom-call | flops 5435817984 | bytes 18874368 | tf_op jit(solution)/shard_map/pallas_call | solution.py:337
  132.1 2.3 %collective-permute-start.33 = (bf16[128,768]{1,0:T(8,128)(2,1)S(1)}, bf16[128,768]{1,0:T(8,128)(2,1)S(1)}, u32[]{:S(2)}, u32[]{:S(2)}) collective-permute-start(bf16[128,768]{1,0:T(8,128)(2,1)S(1)} %fusion.3), channel_id=1, source_target_pairs={{0,4},{4,8},{8,12},{12,0},{1,5},{5,9},{9,13},{13,1},{2,6},{6,10},{... | collective-permute-start | bytes 589832 | tf_op jit(solution)/shard_map/ppermute | solution.py:514
  134.4 1.6 %collective-permute-start.30 = (bf16[128,768]{1,0:T(8,128)(2,1)S(1)}, bf16[128,768]{1,0:T(8,128)(2,1)S(1)}, u32[]{:S(2)}, u32[]{:S(2)}) collective-permute-start(bf16[128,768]{1,0:T(8,128)(2,1)S(1)} %get-tuple-element.94), channel_id=1, source_target_pairs={{0,12},{4,0},{8,4},{12,8},{1,13},{5,1},{9,5},{13,9},{2,14},{6,2},{... | collective-permute-start | bytes 589832 | tf_op jit(solution)/shard_map/ppermute | solution.py:514
  136.0 17.4 %shard_map.111 = (bf16[2,3072,1024]{2,1,0:T(8,128)(2,1)}, bf16[2,3072,1024]{2,1,0:T(8,128)(2,1)}, bf16[2,1024,3072]{2,1,0:T(8,128)(2,1)}) custom-call(bf16[288,3072]{1,0:T(8,128)(2,1)} %get-tuple-element.56.xp_ref, bf16[288,1024]{1,0:T(8,128)(2,1)} %get-tuple-element.57.hid_ref, ...), custom_call_target="tpu_custom_call", output_to_operand_aliasing={{0}: (5, {}), {1}: (6, {}), {2}: (7, {})} | custom-call | flops 5435817984 | bytes 18874368 | tf_op jit(solution)/shard_map/pallas_call | solution.py:337
  (98 shorter events, 13.9 us)
Async XLA Ops:
  1.7 17.7 %collective-permute-start.2 = (bf16[128,384]{1,0:T(8,128)(2,1)S(1)}, bf16[128,384]{1,0:T(8,128)(2,1)S(1)}, u32[]{:S(2)}, u32[]{:S(2)}) collective-permute-start(bf16[128,384]{1,0:T(8,128)(2,1)S(1)} %get-tuple-element.93), channel_id=1, source_target_pairs={{0,12},{4,0},{8,4},{12,8},{1,13},{5,1},{9,5},{13,9},{2,14},{6,2},{... | collective-permute-start | bytes 294920 | tf_op jit(solution)/shard_map/ppermute | solution.py:355
  6.8 12.6 %collective-permute-start.1 = (bf16[128,384]{1,0:T(8,128)(2,1)S(1)}, bf16[128,384]{1,0:T(8,128)(2,1)S(1)}, u32[]{:S(2)}, u32[]{:S(2)}) collective-permute-start(bf16[128,384]{1,0:T(8,128)(2,1)S(1)} %get-tuple-element.93), channel_id=1, source_target_pairs={{0,8},{4,12},{8,0},{12,4},{1,9},{5,13},{9,1},{13,5},{2,10},{6,14},... | collective-permute-start | bytes 294920 | tf_op jit(solution)/shard_map/ppermute | solution.py:355
  6.8 12.6 %collective-permute-start = (bf16[128,384]{1,0:T(8,128)(2,1)S(1)}, bf16[128,384]{1,0:T(8,128)(2,1)S(1)}, u32[]{:S(2)}, u32[]{:S(2)}) collective-permute-start(bf16[128,384]{1,0:T(8,128)(2,1)S(1)} %get-tuple-element.93), channel_id=1, source_target_pairs={{0,4},{4,8},{8,12},{12,0},{1,5},{5,9},{9,13},{13,1},{2,6},{6,10},{... | collective-permute-start | bytes 294920 | tf_op jit(solution)/shard_map/ppermute | solution.py:355
  9.5 4.5 %collective-permute-start.5 = (f32[8,128]{1,0:T(8,128)S(1)}, f32[8,128]{1,0:T(8,128)S(1)}, u32[]{:S(2)}, u32[]{:S(2)}) collective-permute-start(f32[8,128]{1,0:T(8,128)S(1)} %pad_maximum_fusion.4.refs_0_), channel_id=1, source_target_pairs={{0,12},{4,0},{8,4},{12,8},{1,13},{5,1},{9,5},{13,9},{2,14},{6,2},{... | collective-permute-start | bytes 12296 | tf_op jit(solution)/shard_map/ppermute | solution.py:355
  14.0 5.4 %collective-permute-start.3 = (f32[8,128]{1,0:T(8,128)S(1)}, f32[8,128]{1,0:T(8,128)S(1)}, u32[]{:S(2)}, u32[]{:S(2)}) collective-permute-start(f32[8,128]{1,0:T(8,128)S(1)} %pad_maximum_fusion.4.refs_0_), channel_id=1, source_target_pairs={{0,4},{4,8},{8,12},{12,0},{1,5},{5,9},{9,13},{13,1},{2,6},{6,10},{... | collective-permute-start | bytes 12296 | tf_op jit(solution)/shard_map/ppermute | solution.py:355
  19.5 10.8 %collective-permute-start.10 = (bf16[3,128,384]{2,1,0:T(8,128)(2,1)S(1)}, bf16[3,128,384]{2,1,0:T(8,128)(2,1)S(1)}, u32[]{:S(2)}, u32[]{:S(2)}) collective-permute-start(bf16[3,128,384]{2,1,0:T(8,128)(2,1)S(1)} %pad_maximum_fusion.refs_4_.refs_5_), channel_id=1, source_target_pairs={{0,2},{2,0},{1,3},{3,1},{4,6},{6,4},{5,7},{7,5},{8,10},{10,8},{9,1... | collective-permute-start | bytes 884744 | tf_op jit(solution)/shard_map/ppermute | solution.py:360
  21.1 6.1 %collective-permute-start.9 = (bf16[128,384]{1,0:T(8,128)(2,1)S(1)}, bf16[128,384]{1,0:T(8,128)(2,1)S(1)}, u32[]{:S(2)}, u32[]{:S(2)}) collective-permute-start(bf16[128,384]{1,0:T(8,128)(2,1)S(1)} %get-tuple-element.92), channel_id=1, source_target_pairs={{0,12},{4,0},{8,4},{12,8},{1,13},{5,1},{9,5},{13,9},{2,14},{6,2},{... | collective-permute-start | bytes 294920 | tf_op jit(solution)/shard_map/ppermute | solution.py:355
  23.1 7.2 %collective-permute-start.8 = (bf16[128,384]{1,0:T(8,128)(2,1)S(1)}, bf16[128,384]{1,0:T(8,128)(2,1)S(1)}, u32[]{:S(2)}, u32[]{:S(2)}) collective-permute-start(bf16[128,384]{1,0:T(8,128)(2,1)S(1)} %get-tuple-element.92), channel_id=1, source_target_pairs={{0,8},{4,12},{8,0},{12,4},{1,9},{5,13},{9,1},{13,5},{2,10},{6,14},... | collective-permute-start | bytes 294920 | tf_op jit(solution)/shard_map/ppermute | solution.py:355
  23.1 7.2 %collective-permute-start.7 = (bf16[128,384]{1,0:T(8,128)(2,1)S(1)}, bf16[128,384]{1,0:T(8,128)(2,1)S(1)}, u32[]{:S(2)}, u32[]{:S(2)}) collective-permute-start(bf16[128,384]{1,0:T(8,128)(2,1)S(1)} %get-tuple-element.92), channel_id=1, source_target_pairs={{0,4},{4,8},{8,12},{12,0},{1,5},{5,9},{9,13},{13,1},{2,6},{6,10},{... | collective-permute-start | bytes 294920 | tf_op jit(solution)/shard_map/ppermute | solution.py:355
  23.7 20.9 %collective-permute-start.6 = (bf16[3,128,384]{2,1,0:T(8,128)(2,1)S(1)}, bf16[3,128,384]{2,1,0:T(8,128)(2,1)S(1)}, u32[]{:S(2)}, u32[]{:S(2)}) collective-permute-start(bf16[3,128,384]{2,1,0:T(8,128)(2,1)S(1)} %pad_maximum_fusion.refs_4_.refs_5_), channel_id=1, source_target_pairs={{0,1},{1,0},{2,3},{3,2},{4,5},{5,4},{6,7},{7,6},{8,9},{9,8},{10,11... | collective-permute-start | bytes 884744 | tf_op jit(solution)/shard_map/ppermute | solution.py:367
  30.4 14.2 %collective-permute-start.16 = (bf16[3,128,384]{2,1,0:T(8,128)(2,1)S(1)}, bf16[3,128,384]{2,1,0:T(8,128)(2,1)S(1)}, u32[]{:S(2)}, u32[]{:S(2)}) collective-permute-start(bf16[3,128,384]{2,1,0:T(8,128)(2,1)S(1)} %pad_maximum_fusion.1.refs_9_), channel_id=1, source_target_pairs={{0,2},{2,0},{1,3},{3,1},{4,6},{6,4},{5,7},{7,5},{8,10},{10,8},{9,1... | collective-permute-start | bytes 884744 | tf_op jit(solution)/shard_map/ppermute | solution.py:360
  31.0 13.6 %collective-permute-start.11 = (bf16[3,128,384]{2,1,0:T(8,128)(2,1)S(1)}, bf16[3,128,384]{2,1,0:T(8,128)(2,1)S(1)}, u32[]{:S(2)}, u32[]{:S(2)}) collective-permute-start(bf16[3,128,384]{2,1,0:T(8,128)(2,1)S(1)} %get-tuple-element.51.refs_6_.refs_7_), channel_id=1, source_target_pairs={{0,1},{1,0},{2,3},{3,2},{4,5},{5,4},{6,7},{7,6},{8,9},{9,8},{10,11... | collective-permute-start | bytes 884744 | tf_op jit(solution)/shard_map/ppermute | solution.py:367
  31.9 6.2 %collective-permute-start.15 = (bf16[128,384]{1,0:T(8,128)(2,1)S(1)}, bf16[128,384]{1,0:T(8,128)(2,1)S(1)}, u32[]{:S(2)}, u32[]{:S(2)}) collective-permute-start(bf16[128,384]{1,0:T(8,128)(2,1)S(1)} %get-tuple-element.91), channel_id=1, source_target_pairs={{0,12},{4,0},{8,4},{12,8},{1,13},{5,1},{9,5},{13,9},{2,14},{6,2},{... | collective-permute-start | bytes 294920 | tf_op jit(solution)/shard_map/ppermute | solution.py:355
  33.2 7.9 %collective-permute-start.14 = (bf16[128,384]{1,0:T(8,128)(2,1)S(1)}, bf16[128,384]{1,0:T(8,128)(2,1)S(1)}, u32[]{:S(2)}, u32[]{:S(2)}) collective-permute-start(bf16[128,384]{1,0:T(8,128)(2,1)S(1)} %get-tuple-element.91), channel_id=1, source_target_pairs={{0,8},{4,12},{8,0},{12,4},{1,9},{5,13},{9,1},{13,5},{2,10},{6,14},... | collective-permute-start | bytes 294920 | tf_op jit(solution)/shard_map/ppermute | solution.py:355
  38.1 6.4 %collective-permute-start.13 = (bf16[128,384]{1,0:T(8,128)(2,1)S(1)}, bf16[128,384]{1,0:T(8,128)(2,1)S(1)}, u32[]{:S(2)}, u32[]{:S(2)}) collective-permute-start(bf16[128,384]{1,0:T(8,128)(2,1)S(1)} %get-tuple-element.91), channel_id=1, source_target_pairs={{0,4},{4,8},{8,12},{12,0},{1,5},{5,9},{9,13},{13,1},{2,6},{6,10},{... | collective-permute-start | bytes 294920 | tf_op jit(solution)/shard_map/ppermute | solution.py:355
  41.1 6.9 %collective-permute-start.12 = (bf16[3,128,384]{2,1,0:T(8,128)(2,1)S(1)}, bf16[3,128,384]{2,1,0:T(8,128)(2,1)S(1)}, u32[]{:S(2)}, u32[]{:S(2)}) collective-permute-start(bf16[3,128,384]{2,1,0:T(8,128)(2,1)S(1)} %pad_maximum_fusion.1.refs_9_), channel_id=1, source_target_pairs={{0,1},{1,0},{2,3},{3,2},{4,5},{5,4},{6,7},{7,6},{8,9},{9,8},{10,11... | collective-permute-start | bytes 884744 | tf_op jit(solution)/shard_map/ppermute | solution.py:367
  44.6 5.0 %collective-permute-start.17 = (bf16[3,128,384]{2,1,0:T(8,128)(2,1)S(1)}, bf16[3,128,384]{2,1,0:T(8,128)(2,1)S(1)}, u32[]{:S(2)}, u32[]{:S(2)}) collective-permute-start(bf16[3,128,384]{2,1,0:T(8,128)(2,1)S(1)} %get-tuple-element.55.refs_11_), channel_id=1, source_target_pairs={{0,1},{1,0},{2,3},{3,2},{4,5},{5,4},{6,7},{7,6},{8,9},{9,8},{10,11... | collective-permute-start | bytes 884744 | tf_op jit(solution)/shard_map/ppermute | solution.py:367
  44.7 15.2 %collective-permute-start.21 = (bf16[128,384]{1,0:T(8,128)(2,1)S(1)}, bf16[128,384]{1,0:T(8,128)(2,1)S(1)}, u32[]{:S(2)}, u32[]{:S(2)}) collective-permute-start(bf16[128,384]{1,0:T(8,128)(2,1)S(1)} %get-tuple-element.90), channel_id=1, source_target_pairs={{0,12},{4,0},{8,4},{12,8},{1,13},{5,1},{9,5},{13,9},{2,14},{6,2},{... | collective-permute-start | bytes 294920 | tf_op jit(solution)/shard_map/ppermute | solution.py:355
  46.6 13.3 %collective-permute-start.20 = (bf16[128,384]{1,0:T(8,128)(2,1)S(1)}, bf16[128,384]{1,0:T(8,128)(2,1)S(1)}, u32[]{:S(2)}, u32[]{:S(2)}) collective-permute-start(bf16[128,384]{1,0:T(8,128)(2,1)S(1)} %get-tuple-element.90), channel_id=1, source_target_pairs={{0,8},{4,12},{8,0},{12,4},{1,9},{5,13},{9,1},{13,5},{2,10},{6,14},... | collective-permute-start | bytes 294920 | tf_op jit(solution)/shard_map/ppermute | solution.py:355
  46.6 13.3 %collective-permute-start.19 = (bf16[128,384]{1,0:T(8,128)(2,1)S(1)}, bf16[128,384]{1,0:T(8,128)(2,1)S(1)}, u32[]{:S(2)}, u32[]{:S(2)}) collective-permute-start(bf16[128,384]{1,0:T(8,128)(2,1)S(1)} %get-tuple-element.90), channel_id=1, source_target_pairs={{0,4},{4,8},{8,12},{12,0},{1,5},{5,9},{9,13},{13,1},{2,6},{6,10},{... | collective-permute-start | bytes 294920 | tf_op jit(solution)/shard_map/ppermute | solution.py:355
  48.0 11.9 %collective-permute-start.22 = (bf16[3,128,384]{2,1,0:T(8,128)(2,1)S(1)}, bf16[3,128,384]{2,1,0:T(8,128)(2,1)S(1)}, u32[]{:S(2)}, u32[]{:S(2)}) collective-permute-start(bf16[3,128,384]{2,1,0:T(8,128)(2,1)S(1)} %pad_maximum_fusion.2.refs_5_), channel_id=1, source_target_pairs={{0,2},{2,0},{1,3},{3,1},{4,6},{6,4},{5,7},{7,5},{8,10},{10,8},{9,1... | collective-permute-start | bytes 884744 | tf_op jit(solution)/shard_map/ppermute | solution.py:360
  49.6 24.6 %collective-permute-start.18 = (bf16[3,128,384]{2,1,0:T(8,128)(2,1)S(1)}, bf16[3,128,384]{2,1,0:T(8,128)(2,1)S(1)}, u32[]{:S(2)}, u32[]{:S(2)}) collective-permute-start(bf16[3,128,384]{2,1,0:T(8,128)(2,1)S(1)} %pad_maximum_fusion.2.refs_5_), channel_id=1, source_target_pairs={{0,1},{1,0},{2,3},{3,2},{4,5},{5,4},{6,7},{7,6},{8,9},{9,8},{10,11... | collective-permute-start | bytes 884744 | tf_op jit(solution)/shard_map/ppermute | solution.py:367
  61.2 11.3 %collective-permute-start.25 = (bf16[3,128,384]{2,1,0:T(8,128)(2,1)S(1)}, bf16[3,128,384]{2,1,0:T(8,128)(2,1)S(1)}, u32[]{:S(2)}, u32[]{:S(2)}) collective-permute-start(bf16[3,128,384]{2,1,0:T(8,128)(2,1)S(1)} %pad_maximum_fusion.3.refs_9_), channel_id=1, source_target_pairs={{0,2},{2,0},{1,3},{3,1},{4,6},{6,4},{5,7},{7,5},{8,10},{10,8},{9,1... | collective-permute-start | bytes 884744 | tf_op jit(solution)/shard_map/ppermute | solution.py:360
  61.8 13.0 %collective-permute-start.24 = (bf16[3,128,384]{2,1,0:T(8,128)(2,1)S(1)}, bf16[3,128,384]{2,1,0:T(8,128)(2,1)S(1)}, u32[]{:S(2)}, u32[]{:S(2)}) collective-permute-start(bf16[3,128,384]{2,1,0:T(8,128)(2,1)S(1)} %pad_maximum_fusion.3.refs_9_), channel_id=1, source_target_pairs={{0,1},{1,0},{2,3},{3,2},{4,5},{5,4},{6,7},{7,6},{8,9},{9,8},{10,11... | collective-permute-start | bytes 884744 | tf_op jit(solution)/shard_map/ppermute | solution.py:367
  62.0 13.5 %collective-permute-start.23 = (bf16[3,128,384]{2,1,0:T(8,128)(2,1)S(1)}, bf16[3,128,384]{2,1,0:T(8,128)(2,1)}, u32[]{:S(2)}, u32[]{:S(2)}) collective-permute-start(bf16[3,128,384]{2,1,0:T(8,128)(2,1)S(1)} %get-tuple-element.62.refs_7_), channel_id=1, source_target_pairs={{0,1},{1,0},{2,3},{3,2},{4,5},{5,4},{6,7},{7,6},{8,9},{9,8},{10,11... | collective-permute-start | bytes 884744 | tf_op jit(solution)/shard_map/ppermute | solution.py:367
  99.5 12.2 %collective-permute-start.28 = (bf16[4,128,768]{2,1,0:T(8,128)(2,1)}, bf16[4,128,768]{2,1,0:T(8,128)(2,1)S(1)}, u32[]{:S(2)}, u32[]{:S(2)}) collective-permute-start(bf16[4,128,768]{2,1,0:T(8,128)(2,1)} %get-tuple-element.85), channel_id=1, source_target_pairs={{0,1},{1,0},{2,3},{3,2},{4,5},{5,4},{6,7},{7,6},{8,9},{9,8},{10,11... | collective-permute-start | bytes 2359304 | tf_op jit(solution)/shard_map/ppermute | solution.py:488
  111.5 20.1 %collective-permute-start.27 = (bf16[4,128,768]{2,1,0:T(8,128)(2,1)}, bf16[4,128,768]{2,1,0:T(8,128)(2,1)S(1)}, u32[]{:S(2)}, u32[]{:S(2)}) collective-permute-start(bf16[4,128,768]{2,1,0:T(8,128)(2,1)} %get-tuple-element.83), channel_id=1, source_target_pairs={{0,1},{1,0},{2,3},{3,2},{4,5},{5,4},{6,7},{7,6},{8,9},{9,8},{10,11... | collective-permute-start | bytes 2359304 | tf_op jit(solution)/shard_map/ppermute | solution.py:504
  112.0 19.6 %collective-permute-start.29 = (bf16[2,128,768]{2,1,0:T(8,128)(2,1)S(1)}, bf16[2,128,768]{2,1,0:T(8,128)(2,1)S(1)}, u32[]{:S(2)}, u32[]{:S(2)}) collective-permute-start(bf16[2,128,768]{2,1,0:T(8,128)(2,1)S(1)} %get-tuple-element.88), channel_id=1, source_target_pairs={{0,2},{2,0},{1,3},{3,1},{4,6},{6,4},{5,7},{7,5},{8,10},{10,8},{9,1... | collective-permute-start | bytes 1179656 | tf_op jit(solution)/shard_map/ppermute | solution.py:491
  113.5 18.2 %collective-permute-start.32 = (bf16[2,128,768]{2,1,0:T(8,128)(2,1)S(1)}, bf16[2,128,768]{2,1,0:T(8,128)(2,1)S(1)}, u32[]{:S(2)}, u32[]{:S(2)}) collective-permute-start(bf16[2,128,768]{2,1,0:T(8,128)(2,1)S(1)} %get-tuple-element.89), channel_id=1, source_target_pairs={{0,2},{2,0},{1,3},{3,1},{4,6},{6,4},{5,7},{7,5},{8,10},{10,8},{9,1... | collective-permute-start | bytes 1179656 | tf_op jit(solution)/shard_map/ppermute | solution.py:491
  132.1 21.3 %collective-permute-start.33 = (bf16[128,768]{1,0:T(8,128)(2,1)S(1)}, bf16[128,768]{1,0:T(8,128)(2,1)S(1)}, u32[]{:S(2)}, u32[]{:S(2)}) collective-permute-start(bf16[128,768]{1,0:T(8,128)(2,1)S(1)} %fusion.3), channel_id=1, source_target_pairs={{0,4},{4,8},{8,12},{12,0},{1,5},{5,9},{9,13},{13,1},{2,6},{6,10},{... | collective-permute-start | bytes 589832 | tf_op jit(solution)/shard_map/ppermute | solution.py:514
  134.4 19.1 %collective-permute-start.30 = (bf16[128,768]{1,0:T(8,128)(2,1)S(1)}, bf16[128,768]{1,0:T(8,128)(2,1)S(1)}, u32[]{:S(2)}, u32[]{:S(2)}) collective-permute-start(bf16[128,768]{1,0:T(8,128)(2,1)S(1)} %get-tuple-element.94), channel_id=1, source_target_pairs={{0,12},{4,0},{8,4},{12,8},{1,13},{5,1},{9,5},{13,9},{2,14},{6,2},{... | collective-permute-start | bytes 589832 | tf_op jit(solution)/shard_map/ppermute | solution.py:514
  136.0 17.5 %collective-permute-start.31 = (bf16[128,768]{1,0:T(8,128)(2,1)S(1)}, bf16[128,768]{1,0:T(8,128)(2,1)S(1)}, u32[]{:S(2)}, u32[]{:S(2)}) collective-permute-start(bf16[128,768]{1,0:T(8,128)(2,1)S(1)} %get-tuple-element.95), channel_id=1, source_target_pairs={{0,8},{4,12},{8,0},{12,4},{1,9},{5,13},{9,1},{13,5},{2,10},{6,14},... | collective-permute-start | bytes 589832 | tf_op jit(solution)/shard_map/ppermute | solution.py:514
  (18 other events, 130.3 us)
